TPU v7x, 256 devices: a whole 4x4x8 slice. The times are simulated.
256 devices in a mesh: rep: 32 (over x, z), fsdp: 8 (over y, core).
Axes of the slice: x: 4, y: 4, z: 8, core: 2. Of those that a mesh axis runs over, the one named last changes fastest.
Arguments:
- raw_grads: bfloat16 [256, 64, 32768], P(('rep', 'fsdp')), may hold values from -6 to 6
- momentum: float32 [32, 64, 32768], P('rep', None, 'fsdp'), may hold values from -6 to 6
- positions: int32 [512, 32], P('fsdp'), may hold values from 0 to 4095, as said below
Outputs:
- new_momentum: float32 [32, 64, 32768], P('rep', None, 'fsdp')
- update: float32 [64, 32768], P(None, 'fsdp')
Inputs may be any that keep to these rules, and one draw needn't show every extreme that they name: Each row holds 32 different positions.
All inputs are finite; a program needn't handle non-finite values.
Results may differ from a plain program's by a relative error of at most 0.0003.
Values sent between devices are 32-bit elements; how exact they have to be, the bound alone decides.
A program may use at most 128 MiB of HBM per device.

v0:
```python
import math

import jax
import jax.numpy as jnp
from jax import lax
from jax.sharding import PartitionSpec as P

BLOCK = 64


def dct_cosines(order):
    frequency = jnp.arange(order, dtype=jnp.float32)[:, None]
    samples = jnp.arange(order, dtype=jnp.float32)[None, :]
    cosines = jnp.cos(math.pi * (samples + 0.5) * frequency / order) * math.sqrt(2.0 / order)
    return jnp.where(frequency == 0, cosines * math.sqrt(0.5), cosines)


def forward(field, cosines):
    order = cosines.shape[0]
    left = jnp.dot(cosines, field, precision=lax.Precision.HIGHEST)
    blocks = left.reshape(order, -1, order)
    right = jnp.einsum("rnc,kc->rnk", blocks, cosines, precision=lax.Precision.HIGHEST)
    return right.reshape(order, -1)


def inverse(spectrum, cosines):
    order = cosines.shape[0]
    left = jnp.dot(cosines.T, spectrum, precision=lax.Precision.HIGHEST)
    blocks = left.reshape(order, -1, order)
    right = jnp.einsum("rnk,kc->rnc", blocks, cosines, precision=lax.Precision.HIGHEST)
    return right.reshape(order, -1)


def flat_places(positions, order):
    count = positions.shape[0]
    span_ids = jnp.arange(count, dtype=jnp.int32)[:, None]
    return positions // order * (count * order) + span_ids * order + positions % order


def per_device(raw_grads, momentum, positions):
    order = BLOCK
    cosines = dct_cosines(order)
    groups = lax.axis_size("fsdp")
    terms = raw_grads[0].astype(jnp.float32)
    summed = lax.psum_scatter(terms, "fsdp", scatter_dimension=1, tiled=True)
    grads = summed / groups
    moved = 0.999 * momentum[0] + grads
    spectrum = forward(moved, cosines)
    places = flat_places(positions, order).reshape(-1)
    flat = spectrum.reshape(-1)
    shared = flat[places].reshape(positions.shape)
    kept = flat.at[places].set(jnp.float32(0.0)).reshape(spectrum.shape)
    new_momentum = inverse(kept, cosines)[None]
    gathered = lax.all_gather(shared[None], "rep", axis=0, tiled=True)
    total = jnp.sum(gathered, axis=0)
    sparse = jnp.zeros(flat.shape, jnp.float32).at[places].set(total.reshape(-1))
    dense = inverse(sparse.reshape(spectrum.shape), cosines)
    blocks = dense.reshape(order, -1, order)
    scale = jnp.sqrt(jnp.mean(blocks * blocks, axis=(0, 2), keepdims=True) + 1e-06)
    update = jnp.tanh(blocks / scale).reshape(spectrum.shape)
    return (new_momentum, update)


def solution(mesh):
    placed = (P(("rep", "fsdp"), None, None), P("rep", None, "fsdp"), P("fsdp", None))
    return jax.shard_map(
        per_device,
        mesh=mesh,
        in_specs=placed,
        out_specs=(P("rep", None, "fsdp"), P(None, "fsdp")),
        check_vma=False,
    )
```

profile of v0, /device:TPU:8, one launch (start us, length us, event | category | flops | bytes accessed | tf_op | source)
XLA Modules:
  0.0 195.5 jit_solution(12068845648998145509)
XLA Ops:
  7.2 6.0 %bitcast_convert_fusion = f32[64,32768]{1,0:T(8,128)} fusion(bf16[1,64,32768]{2,1,0:T(8,128)(2,1)} %param.3), kind=kLoop, calls=%fused_computation.3 | loop fusion | flops 2097152 | bytes 12582912 | tf_op jit(solution)/shard_map/convert_element_type | solution.py:44
  13.2 0.7 copy-done.1
  14.0 0.1 reshape.84
  14.1 54.7 %reduce-scatter.2.cloned.1.call-done = f32[64,4096]{1,0:T(8,128)} async-done(((f32[64,32768]{1,0:T(8,128)}), f32[64,4096]{1,0:T(8,128)}) %reduce-scatter.2.cloned.1.call-update) | async-done | bytes 1048592 | tf_op jit(solution)/shard_map/reduce_scatter | solution.py:45
  68.8 2.4 %fusion.4 = f32[64,4096]{1,0:T(8,128)S(1)} fusion(f32[64,4096]{1,0:T(8,128)} %reduce-scatter.2.cloned.1.call-done, f32[1,64,4096]{2,1,0:T(8,128)S(1)} %copy-done, f32[64]{0:T(128)S(1)} %add_multiply_fusion, pred[64]{0:T(512)(128)(4,1)S(1)} %iota_compare_fusion), kind=kOutput, calls=%fused_computation.11 | convolution fusion | flops 202133504 | bytes 3146048 | tf_op jit(solution)/shard_map/dot_general | solution.py:20
  71.2 0.8 reshape.83
  72.1 3.3 %fusion.12 = f32[64,64,64]{2,1,0:T(8,128)} fusion(f32[64,64,64]{2,1,0:T(8,128)S(1)} %reshape.83, f32[64]{0:T(128)S(1)} %add_multiply_fusion, pred[64]{0:T(512)(128)(4,1)S(1)} %iota_compare_fusion), kind=kOutput, calls=%fused_computation.20 | convolution fusion | flops 201347072 | bytes 2097472 | tf_op jit(solution)/shard_map/rnc,kc->rnk/dot_general | solution.py:22
  75.4 1.8 reshape_reshape.3
  77.2 11.8 %gather_fusion = f32[2048]{0:T(1024)S(1)} fusion(f32[262144]{0:T(1024)S(1)} %reshape_reshape.3, s32[2048]{0:T(1024)S(1)} %broadcast_clamp_fusion), kind=kCustom, calls=%fused_computation | custom fusion | bytes 24576 | tf_op jit(solution)/shard_map/gather | solution.py:51
  89.1 8.6 %scatter_fusion = f32[262144]{0:T(1024)S(1)} fusion(f32[262144]{0:T(1024)S(1)} %reshape_reshape.3, s32[2048]{0:T(1024)S(1)} %bitcast.34, f32[2048]{0:T(1024)S(1)} %broadcast.70), kind=kCustom, calls=%fused_computation.1 | custom fusion | bytes 32768 | tf_op jit(solution)/shard_map/scatter | solution.py:52
  97.7 0.2 reshape.85
  97.9 0.6 copy.40
  98.5 6.3 %fusion.17 = f32[64,64,64]{2,0,1:T(8,128)S(1)} fusion(f32[64,64,64]{2,1,0:T(8,128)S(1)} %bitcast.29, f32[64]{0:T(128)S(1)} %add_multiply_fusion, pred[64]{0:T(512)(128)(4,1)S(1)} %iota_compare_fusion), kind=kOutput, calls=%fused_computation.25 | convolution fusion | flops 201347072 | bytes 2097472 | tf_op jit(solution)/shard_map/dot_general | solution.py:28
  104.8 3.4 %fusion.2 = f32[64,64,64]{2,1,0:T(8,128)S(1)} fusion(f32[64,64,64]{2,0,1:T(8,128)S(1)} %fusion.17, f32[64]{0:T(128)S(1)} %add_multiply_fusion, pred[64]{0:T(512)(128)(4,1)S(1)} %iota_compare_fusion), kind=kOutput, calls=%fused_computation.6 | convolution fusion | flops 201347072 | bytes 2097472 | tf_op jit(solution)/shard_map/rnk,kc->rnc/dot_general | solution.py:30
  108.2 1.6 broadcast_in_dim_reshape.6
  109.9 50.5 %all_gather.3 = f32[32,64,32]{1,2,0:T(8,128)S(1)} all-gather(f32[1,64,32]{1,2,0:T(8,128)S(1)} %copy.32), channel_id=1, replica_groups=mesh['rep'=32,'fsdp'=8] {'rep'}, dimensions={0}, use_global_device_ids=true | all-gather | bytes 270336 | tf_op jit(solution)/shard_map/all_gather | solution.py:54
  160.6 8.5 %scatter_custom_fusion.1 = f32[262144]{0:T(1024)S(1)} fusion(s32[2048]{0:T(1024)S(1)} %bitcast.35, f32[2048]{0:T(1024)S(1)} %reshape.110, f32[]{:T(128)} %constant.22.clone.1), kind=kCustom, calls=%fused_computation.14 | custom fusion | bytes 1048580 | tf_op jit(solution)/shard_map/scatter | solution.py:56
  169.2 0.2 reshape.87
  169.4 0.6 copy.42
  170.0 6.3 %fusion.15 = f32[64,64,64]{2,0,1:T(8,128)S(1)} fusion(f32[64,64,64]{2,1,0:T(8,128)S(1)} %bitcast.30, f32[64]{0:T(128)S(1)} %add_multiply_fusion, pred[64]{0:T(512)(128)(4,1)S(1)} %iota_compare_fusion), kind=kOutput, calls=%fused_computation.23 | convolution fusion | flops 201347072 | bytes 2097472 | tf_op jit(solution)/shard_map/dot_general | solution.py:28
  176.3 7.1 %multiply_reduce_fusion = (f32[64]{0:T(128)S(1)}, f32[64,64,64]{1,2,0:T(8,128)S(1)}) fusion(f32[64]{0:T(128)S(1)} %add_multiply_fusion, pred[64]{0:T(512)(128)(4,1)S(1)} %iota_compare_fusion, f32[64,64,64]{2,0,1:T(8,128)S(1)} %fusion.15), kind=kOutput, calls=%fused_computation.9 | convolution fusion | flops 201871296 | bytes 2097728 | tf_op jit(solution)/shard_map/rnk,kc->rnc/dot_general | solution.py:30
  183.4 0.5 divide_tanh_fusion
  183.9 1.9 copy.36
  185.7 2.9 %reshape.88 = f32[64,4096]{1,0:T(8,128)} reshape(f32[64,64,64]{2,1,0:T(8,128)} %copy.36) | data formatting | bytes 2097152 | tf_op jit(solution)/shard_map/reshape | solution.py:60
  (19 shorter events, 0.6 us)
Async XLA Ops:
  7.2 61.6 %reduce-scatter.2.cloned.1.call-start = ((), (), s32[]{:S(2)}) async-start(), calls=%async_computation.1 | async-start | bytes 9437184 | tf_op jit(solution)/shard_map/reduce_scatter | solution.py:45
  13.2 0.7 copy-start.1
  13.2 55.6 %copy-start = (f32[1,64,4096]{2,1,0:T(8,128)S(1)}, f32[1,64,4096]{2,1,0:T(8,128)}, u32[]{:S(2)}) copy-start(f32[1,64,4096]{2,1,0:T(8,128)} %param.4) | copy-start | bytes 3145732
Sparse Core Ops, SparseCore 0:
  13.3 55.4 reduce-scatter.1
where the time goes:
time: 197 us; the launch traced here: 195 us
  waiting for transfers between devices  54.7 us (28%)
  blocking collectives  50.5 us (26%)
  local copies, waits for them, and re-layouts  40.7 us (21%)
  matrix products  28.8 us (15%)
  between operations  14.2 us (7%)
  other arithmetic  6.57 us (3%)
    reduce_scatter x1, waiting for transfers between devices, per_device(): summed = lax.psum_scatter(terms, 'fsdp', scatter_dimension=1, tiled=True)  54.7 us
    all_gather x1, blocking collectives, per_device(): gathered = lax.all_gather(shared[None], 'rep', axis=0, tiled=True)  50.5 us
    dot_general x2, matrix products, inverse(): left = jnp.dot(cosines.T, spectrum, precision=lax.Precision.HIGHEST)  12.6 us
    gather x1, local copies, waits for them, and re-layouts, per_device(): shared = flat[places].reshape(positions.shape)  11.8 us
    dot_general x2, matrix products, inverse(): jnp.einsum('rnk,kc->rnc', blocks, cosines, precision=lax.Precision.HIGHEST)  10.5 us
    scatter x1, local copies, waits for them, and re-layouts, per_device(): kept = flat.at[places].set(jnp.float32(0.0)).reshape(spectrum.shape)  8.65 us
    scatter x1, local copies, waits for them, and re-layouts, per_device(): jnp.zeros(flat.shape, jnp.float32).at[places].set(total.reshape(-1))  8.55 us
    convert_element_type x1, other arithmetic, per_device(): terms = raw_grads[0].astype(jnp.float32)  5.96 us
  transfers between devices with their start and end apart: 1, of which 1 were waited for; matrix products, arithmetic and copies ran while one was open for 0% of the time, Pallas kernels for 0%

commit v1 on v0

v1 whole, which is shorter than its diff:
```python
import math

import jax
import jax.numpy as jnp
import ml_dtypes
import numpy as np
from jax import lax
from jax.experimental import pallas as pl
from jax.experimental.pallas import tpu as pltpu
from jax.sharding import PartitionSpec as P

MESH = pl.DeviceIdType.MESH
F32, BF16 = jnp.float32, jnp.bfloat16

BLOCK = 64
KEEP = 32
X, Y, Z, CORES = 4, 4, 8, 2
WIDTH = 4096
PIECES = 8
HALF = PIECES // 2
COLS = WIDTH // PIECES
SPANS = COLS // BLOCK
ROWS = SPANS * KEEP
TILES = PIECES * SPANS * KEEP // (8 * 128)
AHEAD, BEHIND, ACROSS = 1, 3, 2


def dct_tables():
    k = np.arange(BLOCK)[:, None]
    j = np.arange(BLOCK)[None, :]
    cosines = np.cos(np.pi * (j + 0.5) * k / BLOCK) * math.sqrt(2.0 / BLOCK)
    cosines = np.where(k == 0, cosines * math.sqrt(0.5), cosines)
    high = cosines.astype(ml_dtypes.bfloat16)
    low = (cosines - high.astype(np.float64)).astype(ml_dtypes.bfloat16)
    return np.concatenate([high, low], axis=1)


def split(x):
    high = x.astype(BF16)
    return high, (x - high.astype(F32)).astype(BF16)


def lanes(shape):
    return lax.broadcasted_iota(jnp.int32, shape, 1)


def own_lane(piece):
    row = lax.broadcasted_iota(jnp.int32, (ROWS, 128), 0)
    return lanes((ROWS, 128)) == lax.rem(row, KEEP) + KEEP * lax.rem(piece, 4)


def unpack(tile, piece):
    wide = jnp.broadcast_to(tile[:, None, :], (SPANS, KEEP, 128)).reshape(ROWS, 128)
    return jnp.sum(jnp.where(own_lane(piece), wide, 0.0), axis=1, keepdims=True)


def pack(column, piece):
    wide = jnp.where(own_lane(piece), column, 0.0)
    return jnp.sum(wide.reshape(SPANS, KEEP, 128), axis=1)


def kernel(
    raw, mom, pos, cos, out_m, out_u,
    raw_v, mom_v, pos_v, cos_v, xsend, part, ya, yb, yc, base, out_v, upd_v,
    places, left, right, left_t, csend, crecv, xslots, zslots,
    raw_sem, in_sem, x_send_sem, x_recv_sem, y_send_sem, y_recv_sem,
    p_send_sem, p_recv_sem, c_send_sem, c_recv_sem,
    rx_send_sem, rx_recv_sem, rz_send_sem, rz_recv_sem, out_sem,
):
    rep, fs = lax.axis_index("rep"), lax.axis_index("fsdp")
    y, core = fs // CORES, lax.rem(fs, CORES)
    x, z = rep // Z, lax.rem(rep, Z)

    def y_peer(step):
        return (rep, lax.rem(y + step, Y) * CORES + core)

    def x_peer(step):
        return (lax.rem(x + step, X) * Z + z, fs)

    def z_peer(step):
        return (x * Z + lax.rem(z + step, Z), fs)

    sibling = (rep, y * CORES + 1 - core)
    peers = [sibling, y_peer(AHEAD), y_peer(BEHIND)]
    peers += [x_peer(s) for s in range(1, X)] + [z_peer(s) for s in range(1, Z)]
    barrier = pltpu.get_barrier_semaphore()
    for peer in peers:
        pl.semaphore_signal(barrier, inc=1, device_id=peer, device_id_type=MESH)

    def raw_copy(k, slot):
        owner = lax.rem(y + k, Y) * CORES + (core if slot == 0 else 1 - core)
        start = pl.multiple_of(owner * WIDTH, WIDTH)
        return pltpu.make_async_copy(
            raw.at[0, :, pl.ds(start, WIDTH)], raw_v.at[k, slot], raw_sem.at[k, slot])

    order = (ACROSS, BEHIND, AHEAD, 0)
    for k in order:
        raw_copy(k, 1).start()
        raw_copy(k, 0).start()
    pos_copy = pltpu.make_async_copy(pos, pos_v, in_sem.at[0])
    cos_copy = pltpu.make_async_copy(cos, cos_v, in_sem.at[1])
    mom_copy = pltpu.make_async_copy(mom.at[0], mom_v, in_sem.at[2])
    pos_copy.start()
    cos_copy.start()
    mom_copy.start()
    pl.semaphore_wait(barrier, len(peers))

    def columns(piece):
        return pl.ds(pl.multiple_of(piece * COLS, COLS), COLS)

    def x_copy(k, p):
        return pltpu.make_async_remote_copy(
            xsend.at[k, p], part.at[k, p], x_send_sem.at[k, p], x_recv_sem.at[k, p],
            device_id=sibling, device_id_type=MESH)

    def to_sibling(k, p):
        xsend[k, p] = raw_v[k, 1, :, columns(p)].astype(F32)
        x_copy(k, p).start()

    for k in order:
        raw_copy(k, 1).wait()

        @pl.loop(0, HALF)
        def _(i):
            to_sibling(k, i)
            to_sibling(k, HALF + i)

        raw_copy(k, 0).wait()

    def y_copy(stage, way, i, src):
        dst = (ya, yb, yc)[stage]
        return pltpu.make_async_remote_copy(
            src, dst.at[way, i], y_send_sem.at[stage, way, i], y_recv_sem.at[stage, way, i],
            device_id=y_peer((BEHIND, AHEAD)[way]), device_id_type=MESH)

    def add_sibling(k, p):
        x_copy(k, p).wait_recv()
        part[k, p] = part[k, p] + raw_v[k, 0, :, columns(p)].astype(F32)

    def source(stage, way, i):
        if stage == 0:
            return ACROSS, (i, HALF + i)[way]
        if stage == 1:
            return (BEHIND, AHEAD)[way], (HALF + i, i)[way]
        return (BEHIND, AHEAD)[way], (i, HALF + i)[way]

    for stage in range(2):
        @pl.loop(0, HALF)
        def _(i):
            for way in range(2):
                k, p = source(stage, way, i)
                add_sibling(k, p)
                y_copy(stage, way, i, part.at[k, p]).start()

    pos_copy.wait()
    cos_copy.wait()
    for m in range(TILES):
        places[0, m] = jnp.concatenate(
            [pos_v[pl.ds(8 * (4 * m + j), 8), :] for j in range(4)], axis=1).astype(F32)

    def p_copy(way):
        return pltpu.make_async_remote_copy(
            places.at[0], places.at[1 + way], p_send_sem.at[way], p_recv_sem.at[way],
            device_id=y_peer((AHEAD, BEHIND)[way]), device_id_type=MESH)

    for way in range(2):
        p_copy(way).start()

    @pl.loop(0, HALF)
    def _(i):
        for way in range(2):
            add_sibling(*source(2, way, i))

    mom_copy.wait()

    @pl.loop(0, PIECES)
    def _(p):
        x_copy(0, p).wait_recv()
        total = part[0, p] + raw_v[0, 0, :, columns(p)].astype(F32)
        base[p] = 0.999 * mom_v[:, columns(p)] + total * 0.125

    def prepare(who, p, transposed):
        place = unpack(places[who, p // 4], p).astype(jnp.int32)
        column = lanes((ROWS, BLOCK))
        pick_row = jnp.where(column == lax.shift_right_logical(place, 6), 1.0, 0.0)
        pick_col = jnp.where(column == lax.bitwise_and(place, 63), 1.0, 0.0)
        rows = jnp.dot(pick_row.astype(BF16), cos_v[...], preferred_element_type=F32)
        cols = jnp.dot(pick_col.astype(BF16), cos_v[...], preferred_element_type=F32)
        lane = lanes((ROWS, 128))
        turned = pltpu.roll(rows, 64, 1)
        left[who, p, :, 0:128] = jnp.where(lane < 64, rows, turned).astype(BF16)
        left[who, p, :, 128:256] = jnp.where(lane < 64, turned, rows).astype(BF16)
        odd = lax.rem(lax.broadcasted_iota(jnp.int32, (ROWS, 128), 0) // KEEP, 2)
        both = cols + pltpu.roll(cols, 64, 1)
        right[who, p] = jnp.where(lane // 64 == odd, both, 0.0)
        if transposed:
            for q in range(SPANS // 2):
                flat = rows[64 * q:64 * q + 64].T
                high, low = flat[0:64].astype(BF16), flat[64:128].astype(BF16)
                left_t[p, q] = jnp.concatenate([high, high, low, low], axis=1)

    @pl.loop(0, PIECES)
    def _(p):
        prepare(0, p, True)

    def coefficients(field, who, p):
        found = []
        for h in range(2):
            high, low = split(field[:, 256 * h:256 * h + 256])
            spread = jnp.concatenate([high, low, high, low], axis=0)
            t = jnp.dot(left[who, p, 128 * h:128 * h + 128, :], spread, preferred_element_type=F32)
            t = jnp.concatenate([t[0:64, 0:128], t[64:128, 128:256]], axis=0)
            found.append(jnp.sum(t * right[who, p, 128 * h:128 * h + 128, :], axis=1, keepdims=True))
        return jnp.concatenate(found, axis=0)

    xslots[x] = jnp.zeros((TILES, 8, 128), F32)
    csend[...] = jnp.zeros((2, TILES, 8, 128), F32)

    @pl.loop(0, PIECES)
    def _(p):
        xslots[x, p // 4] += pack(coefficients(base[p], 0, p), p)

    for way in range(2):
        p_copy(way).wait_recv()

    @pl.loop(0, PIECES)
    def _(p):
        prepare(1, p, False)
        prepare(2, p, False)

    def add_coefficients(way, k, p):
        csend[way, p // 4] += pack(coefficients(part[k, p], (1, 2)[way], p), p)

    @pl.loop(0, HALF)
    def _(i):
        for way in range(2):
            add_coefficients(way, *source(1, way, i))

    @pl.loop(0, HALF)
    def _(i):
        for way in range(2):
            k, p = source(2, way, i)
            y_copy(0, way, i, ya.at[way, i]).wait_recv()
            part[k, p] = part[k, p] + ya[way, i]
            y_copy(2, way, i, part.at[k, p]).start()
            add_coefficients(way, k, p)

    def c_copy(way):
        return pltpu.make_async_remote_copy(
            csend.at[way], crecv.at[way], c_send_sem.at[way], c_recv_sem.at[way],
            device_id=y_peer((BEHIND, AHEAD)[way]), device_id_type=MESH)

    for way in range(2):
        c_copy(way).start()
    for way in range(2):
        c_copy(way).wait_recv()
    xslots[x] = xslots[x] + (crecv[0] + crecv[1]) * 0.125

    def rx_copy(step):
        return pltpu.make_async_remote_copy(
            xslots.at[x], xslots.at[x], rx_send_sem.at[step - 1], rx_recv_sem.at[step - 1],
            device_id=x_peer(step), device_id_type=MESH)

    def rz_copy(step):
        return pltpu.make_async_remote_copy(
            zslots.at[z], zslots.at[z], rz_send_sem.at[step - 1], rz_recv_sem.at[step - 1],
            device_id=z_peer(step), device_id_type=MESH)

    for step in range(1, X):
        rx_copy(step).start()

    def inverse(p, q, column):
        high, low = split(column * right[0, p, 64 * q:64 * q + 64, :])
        spread = jnp.concatenate([high, low, high, low], axis=0)
        return jnp.dot(left_t[p, q], spread, preferred_element_type=F32)

    @pl.loop(0, PIECES)
    def _(p):
        column = unpack(xslots[x, p // 4], p)
        for q in range(SPANS // 2):
            base[p, :, 128 * q:128 * q + 128] -= inverse(p, q, column[64 * q:64 * q + 64])

    for step in range(1, X):
        rx_copy(step).wait_recv()
    zslots[z] = (xslots[0] + xslots[1]) + (xslots[2] + xslots[3])
    for step in range(1, Z):
        rz_copy(step).start()
    for step in range(1, Z):
        rz_copy(step).wait_recv()
    zslots_sum = zslots[0]
    for s in range(1, Z):
        zslots_sum = zslots_sum + zslots[s]
    crecv[0] = zslots_sum

    @pl.loop(0, PIECES)
    def _(p):
        column = unpack(crecv[0, p // 4], p)
        mean = jnp.sum((column * column).reshape(SPANS, KEEP, 1), axis=1, keepdims=True)
        scale = 1.0 / jnp.sqrt(mean * (1.0 / (BLOCK * BLOCK)) + 1e-06)
        column = column * jnp.broadcast_to(scale, (SPANS, KEEP, 1)).reshape(ROWS, 1)
        for q in range(SPANS // 2):
            upd_v[p, :, 128 * q:128 * q + 128] = jnp.tanh(inverse(p, q, column[64 * q:64 * q + 64]))
        pltpu.make_async_copy(upd_v.at[p], out_u.at[:, columns(p)], out_sem.at[0, p]).start()

    @pl.loop(0, HALF)
    def _(i):
        for way in range(2):
            p = (HALF + i, i)[way]
            y_copy(1, way, i, yb.at[way, i]).wait_recv()
            base[p] += yb[way, i] * 0.125

    @pl.loop(0, HALF)
    def _(i):
        for way in range(2):
            p = (i, HALF + i)[way]
            y_copy(2, way, i, yc.at[way, i]).wait_recv()
            out_v[p] = base[p] + yc[way, i] * 0.125
            pltpu.make_async_copy(out_v.at[p], out_m.at[0, :, columns(p)], out_sem.at[1, p]).start()

    for way in range(2):
        p_copy(way).wait_send()
        c_copy(way).wait_send()
    for step in range(1, X):
        rx_copy(step).wait_send()
    for step in range(1, Z):
        rz_copy(step).wait_send()

    @pl.loop(0, PIECES)
    def _(p):
        for k in range(Y):
            x_copy(k, p).wait_send()

    @pl.loop(0, HALF)
    def _(i):
        for stage in range(3):
            for way in range(2):
                y_copy(stage, way, i, ya.at[way, i]).wait_send()

    @pl.loop(0, PIECES)
    def _(p):
        pltpu.make_async_copy(upd_v.at[p], out_u.at[:, columns(p)], out_sem.at[0, p]).wait()
        pltpu.make_async_copy(out_v.at[p], out_m.at[0, :, columns(p)], out_sem.at[1, p]).wait()


def per_device(raw_grads, momentum, positions):
    piece = (BLOCK, COLS)
    tiles = (TILES, 8, 128)
    dma = pltpu.SemaphoreType.DMA
    return pl.pallas_call(
        kernel,
        out_shape=(
            jax.ShapeDtypeStruct((1, BLOCK, WIDTH), F32),
            jax.ShapeDtypeStruct((BLOCK, WIDTH), F32),
        ),
        in_specs=[pl.BlockSpec(memory_space=pl.ANY)] * 4,
        out_specs=(pl.BlockSpec(memory_space=pl.ANY), pl.BlockSpec(memory_space=pl.ANY)),
        scratch_shapes=[
            pltpu.VMEM((Y, 2, BLOCK, WIDTH), BF16),
            pltpu.VMEM((BLOCK, WIDTH), F32),
            pltpu.VMEM((WIDTH // BLOCK, KEEP), jnp.int32),
            pltpu.VMEM((BLOCK, 2 * BLOCK), BF16),
            pltpu.VMEM((Y, PIECES) + piece, F32),
            pltpu.VMEM((Y, PIECES) + piece, F32),
            pltpu.VMEM((2, HALF) + piece, F32),
            pltpu.VMEM((2, HALF) + piece, F32),
            pltpu.VMEM((2, HALF) + piece, F32),
            pltpu.VMEM((PIECES,) + piece, F32),
            pltpu.VMEM((PIECES,) + piece, F32),
            pltpu.VMEM((PIECES,) + piece, F32),
            pltpu.VMEM((3,) + tiles, F32),
            pltpu.VMEM((3, PIECES, ROWS, 256), BF16),
            pltpu.VMEM((3, PIECES, ROWS, 128), F32),
            pltpu.VMEM((PIECES, SPANS // 2, BLOCK, 256), BF16),
            pltpu.VMEM((2,) + tiles, F32),
            pltpu.VMEM((2,) + tiles, F32),
            pltpu.VMEM((X,) + tiles, F32),
            pltpu.VMEM((Z,) + tiles, F32),
            dma((Y, 2)), dma((3,)),
            dma((Y, PIECES)), dma((Y, PIECES)),
            dma((3, 2, HALF)), dma((3, 2, HALF)),
            dma((2,)), dma((2,)), dma((2,)), dma((2,)),
            dma((X - 1,)), dma((X - 1,)), dma((Z - 1,)), dma((Z - 1,)),
            dma((2, PIECES)),
        ],
        compiler_params=pltpu.CompilerParams(
            collective_id=0, has_side_effects=True, vmem_limit_bytes=48 * 1024 * 1024),
    )(raw_grads, momentum, positions, dct_tables())


def solution(mesh):
    placed = (P(("rep", "fsdp"), None, None), P("rep", None, "fsdp"), P("fsdp", None))
    return jax.shard_map(
        per_device,
        mesh=mesh,
        in_specs=placed,
        out_specs=(P("rep", None, "fsdp"), P(None, "fsdp")),
        check_vma=False,
    )
```

time: 197 us -> 72.1 us (0.37)
  Pallas kernels: 0 us -> 66.5 us
  waiting for transfers between devices: 54.7 us -> 0 us
  blocking collectives: 50.5 us -> 0 us
  local copies, waits for them, and re-layouts: 40.7 us -> 4.68 us
  matrix products: 28.8 us -> 0 us
  between operations: 14.2 us -> 0.64 us
  other arithmetic: 6.57 us -> 0 us
    pallas_call x0 -> x1, Pallas kernels: none -> 66.5 us  [per_device(): pl.pallas_call(kernel, out_shape=(jax.ShapeDtypeStruct((1, BLOCK, WIDTH),...]
    reduce_scatter x1 -> x0, waiting for transfers between devices: 54.7 us -> none  [per_device(): summed = lax.psum_scatter(terms, 'fsdp', scatter_dimension=1, tiled=True)]
    all_gather x1 -> x0, blocking collectives: 50.5 us -> none  [per_device(): gathered = lax.all_gather(shared[None], 'rep', axis=0, tiled=True)]
    dot_general x6 -> x0, matrix products: 28.8 us -> none  [the longest x2 12.6 us: inverse(): left = jnp.dot(cosines.T, spectrum, precision=lax.Precision.HIGHEST)]
    scatter x2 -> x0, local copies, waits for them, and re-layouts: 17.2 us -> none  [the longest x1 8.65 us: per_device(): kept = flat.at[places].set(jnp.float32(0.0)).reshape(spectrum.shape)]
    gather x1 -> x0, local copies, waits for them, and re-layouts: 11.8 us -> none  [per_device(): shared = flat[places].reshape(positions.shape)]
    convert_element_type x1 -> x0, other arithmetic: 5.96 us -> none  [per_device(): terms = raw_grads[0].astype(jnp.float32)]
    reshape x6 -> x0, local copies, waits for them, and re-layouts: 4.25 us -> none  [the longest x1 2.88 us: per_device(): update = jnp.tanh(blocks / scale).reshape(spectrum.shape)]
  transfers between devices with their start and end apart: 1 -> 0, of which waited for: 1 -> 0; matrix products, arithmetic and copies ran while one was open for 0% -> 0% of each run, Pallas kernels for 0% -> 0%
where the time goes in v1:
time: 72.1 us; the launch traced here: 71.8 us
  Pallas kernels  66.5 us (92%)
  local copies, waits for them, and re-layouts  4.68 us (6%)
    pallas_call x1, Pallas kernels, per_device(): pl.pallas_call(kernel, out_shape=(jax.ShapeDtypeStruct((1, BLOCK, WIDTH),...  66.5 us
    unnamed x7, local copies, waits for them, and re-layouts  4.68 us

profile of v1, /device:TPU:8, one launch (start us, length us, event | category | flops | bytes accessed | tf_op | source)
XLA Modules:
  0.0 71.8 jit_solution(5032246903862815838)
XLA Ops:
  0.6 0.8 %copy.6.pos = s32[64,32]{1,0:T(8,128)S(1)} copy(s32[64,32]{0,1:T(8,128)} %param.6) | data formatting | bytes 16384 | tf_op args[2]
  1.4 0.0 copy-start
  1.4 1.2 %copy-done = f32[1,64,4096]{2,1,0:T(8,128)S(1)} copy-done((f32[1,64,4096]{2,1,0:T(8,128)S(1)}, f32[1,64,4096]{2,1,0:T(8,128)}, u32[]{:S(2)}) %copy-start) | copy-done | bytes 1048600
  2.7 0.0 copy-start.1
  2.7 0.7 copy-done.1
  3.4 66.5 %shard_map.59 = (f32[1,64,4096]{2,1,0:T(8,128)S(1)}, f32[64,4096]{1,0:T(8,128)S(1)}) custom-call(bf16[1,64,32768]{2,1,0:T(8,128)(2,1)} %raw.1, f32[1,64,4096]{2,1,0:T(8,128)S(1)} %copy-done, s32[64,32]{1,0:T(8,128)S(1)} %copy.6.pos, bf16[64,128]{1,0:T(8,128)(2,1)S(1)} %copy-done.1), custom_call_target="tpu_custom_call" | custom-call | tf_op jit(solution)/shard_map/pallas_call | solution.py:349
  69.9 1.0 %copy.9 = f32[1,64,4096]{2,1,0:T(8,128)} copy(f32[1,64,4096]{2,1,0:T(8,128)S(1)} %get-tuple-element.4) | data formatting | bytes 2097152
  70.8 1.0 %copy.10 = f32[64,4096]{1,0:T(8,128)} copy(f32[64,4096]{1,0:T(8,128)S(1)} %get-tuple-element.5) | data formatting | bytes 2097152
Async XLA Ops:
  1.4 1.2 %copy-start = (f32[1,64,4096]{2,1,0:T(8,128)S(1)}, f32[1,64,4096]{2,1,0:T(8,128)}, u32[]{:S(2)}) copy-start(f32[1,64,4096]{2,1,0:T(8,128)} %mom.1) | copy-start | bytes 3145732
  2.7 0.7 copy-start.1

commit v2 on v1

v2 whole, which is shorter than its diff:
```python
import math

import jax
import jax.numpy as jnp
import ml_dtypes
import numpy as np
from jax import lax
from jax.experimental import pallas as pl
from jax.experimental.pallas import tpu as pltpu
from jax.sharding import PartitionSpec as P

MESH = pl.DeviceIdType.MESH
F32, BF16 = jnp.float32, jnp.bfloat16

BLOCK = 64
KEEP = 32
X, Y, Z, CORES = 4, 4, 8, 2
WIDTH = 4096
PIECES = 8
HALF = PIECES // 2
COLS = WIDTH // PIECES
SPANS = COLS // BLOCK
ROWS = SPANS * KEEP
TILES = PIECES * SPANS * KEEP // (8 * 128)
AHEAD, BEHIND, ACROSS = 1, 3, 2
EARLY = 2


def dct_tables():
    k = np.arange(BLOCK)[:, None]
    j = np.arange(BLOCK)[None, :]
    cosines = np.cos(np.pi * (j + 0.5) * k / BLOCK) * math.sqrt(2.0 / BLOCK)
    cosines = np.where(k == 0, cosines * math.sqrt(0.5), cosines)
    high = cosines.astype(ml_dtypes.bfloat16)
    low = (cosines - high.astype(np.float64)).astype(ml_dtypes.bfloat16)
    return np.concatenate([high, low], axis=1)


def split(x):
    high = x.astype(BF16)
    return high, (x - high.astype(F32)).astype(BF16)


def lanes(shape):
    return lax.broadcasted_iota(jnp.int32, shape, 1)


def own_lane(piece):
    row = lax.broadcasted_iota(jnp.int32, (ROWS, 128), 0)
    return lanes((ROWS, 128)) == lax.rem(row, KEEP) + KEEP * lax.rem(piece, 4)


def unpack(tile, piece):
    wide = jnp.broadcast_to(tile[:, None, :], (SPANS, KEEP, 128)).reshape(ROWS, 128)
    return jnp.sum(jnp.where(own_lane(piece), wide, 0.0), axis=1, keepdims=True)


def pack(column, piece):
    wide = jnp.where(own_lane(piece), column, 0.0)
    return jnp.sum(wide.reshape(SPANS, KEEP, 128), axis=1)


def kernel(
    raw, mom, pos, cos, out_m, out_u,
    raw_v, mom_v, pos_v, cos_v, xsend, part, ya, yb, yc, base,
    places, left, right, left_t, csend, crecv, xslots, zslots, total,
    raw_sem, in_sem, go_sem, x_send_sem, x_recv_sem, y_send_sem, y_recv_sem,
    p_send_sem, p_recv_sem, c_send_sem, c_recv_sem,
    rx_send_sem, rx_recv_sem, rz_send_sem, rz_recv_sem, pair_send_sem, pair_recv_sem,
):
    rep, fs = lax.axis_index("rep"), lax.axis_index("fsdp")
    y, core = fs // CORES, lax.rem(fs, CORES)
    x, z = rep // Z, lax.rem(rep, Z)

    def y_peer(step, of=core):
        return (rep, lax.rem(y + step, Y) * CORES + of)

    def x_peer(step):
        return (lax.rem(x + step, X) * Z + z, fs)

    def z_peer(step):
        return (x * Z + lax.rem(z + step, Z), fs)

    sibling = (rep, y * CORES + 1 - core)

    barrier = pltpu.get_barrier_semaphore()

    def greet(peer):
        pl.semaphore_signal(barrier, inc=1, device_id=peer, device_id_type=MESH)

    greet(y_peer(AHEAD, 1))
    greet(y_peer(BEHIND, 1))

    @pl.when(core == 0)
    def _():
        greet(sibling)
        for step in range(1, X):
            greet(x_peer(step))
        for step in range(1, Z):
            greet(z_peer(step))

    def raw_copy(k, slot):
        owner = lax.rem(y + k, Y) * CORES + (core if slot == 0 else 1 - core)
        start = pl.multiple_of(owner * WIDTH, WIDTH)
        return pltpu.make_async_copy(
            raw.at[0, :, pl.ds(start, WIDTH)], raw_v.at[k, slot], raw_sem.at[k, slot])

    order = (ACROSS, BEHIND, AHEAD, 0)
    raw_copy(ACROSS, 1).start()
    raw_copy(ACROSS, 0).start()
    pos_copy = pltpu.make_async_copy(pos, pos_v, in_sem.at[0])
    cos_copy = pltpu.make_async_copy(cos, cos_v, in_sem.at[1])
    mom_copy = pltpu.make_async_copy(mom.at[0], mom_v, in_sem.at[2])
    pos_copy.start()
    cos_copy.start()
    for k in order[1:]:
        raw_copy(k, 1).start()
        raw_copy(k, 0).start()
    mom_copy.start()

    def columns(piece):
        return pl.ds(pl.multiple_of(piece * COLS, COLS), COLS)

    def x_copy(k, p):
        return pltpu.make_async_remote_copy(
            xsend.at[k, p], part.at[k, p], x_send_sem.at[k, p], x_recv_sem.at[k, p],
            device_id=sibling, device_id_type=MESH)

    def widen(k, p):
        xsend[k, p] = raw_v[k, 1, :, columns(p)].astype(F32)

    raw_copy(ACROSS, 1).wait()

    @pl.loop(0, PIECES)
    def _(p):
        widen(ACROSS, p)

    @pl.when(core == 1)
    def _():
        pl.semaphore_wait(barrier, 5)
        pl.semaphore_signal(go_sem, inc=1, device_id=sibling, device_id_type=MESH)

    @pl.when(core == 0)
    def _():
        pl.semaphore_wait(go_sem, 1)

    @pl.loop(0, HALF)
    def _(i):
        x_copy(ACROSS, i).start()
        x_copy(ACROSS, HALF + i).start()

    pos_copy.wait()
    found = pos_v[...].astype(F32).T
    for m in range(TILES):
        places[0, m] = jnp.concatenate(
            [found[8 * (4 * m + j):8 * (4 * m + j) + 8] for j in range(4)], axis=1)

    def p_copy(way):
        return pltpu.make_async_remote_copy(
            places.at[0], places.at[1 + way], p_send_sem.at[way], p_recv_sem.at[way],
            device_id=y_peer((AHEAD, BEHIND)[way]), device_id_type=MESH)

    for way in range(2):
        p_copy(way).start()

    for k in order[1:]:
        raw_copy(k, 1).wait()

        @pl.loop(0, HALF)
        def _(i):
            for p in (i, HALF + i):
                widen(k, p)
                x_copy(k, p).start()

    def y_copy(stage, way, i, src):
        dst = (ya, yb, yc)[stage]
        return pltpu.make_async_remote_copy(
            src, dst.at[way, i], y_send_sem.at[stage, way, i], y_recv_sem.at[stage, way, i],
            device_id=y_peer((BEHIND, AHEAD)[way]), device_id_type=MESH)

    def add_sibling(k, p):
        x_copy(k, p).wait_recv()
        part[k, p] = part[k, p] + raw_v[k, 0, :, columns(p)].astype(F32)

    def source(stage, way, i):
        if stage == 0:
            return ACROSS, (i, HALF + i)[way]
        if stage == 1:
            return (BEHIND, AHEAD)[way], (HALF + i, i)[way]
        return (BEHIND, AHEAD)[way], (i, HALF + i)[way]

    def prepare(who, p, transposed):
        place = unpack(places[who, p // 4], p).astype(jnp.int32)
        column = lanes((ROWS, BLOCK))
        pick_row = jnp.where(column == lax.shift_right_logical(place, 6), 1.0, 0.0)
        pick_col = jnp.where(column == lax.bitwise_and(place, 63), 1.0, 0.0)
        rows = jnp.dot(pick_row.astype(BF16), cos_v[...], preferred_element_type=F32)
        cols = jnp.dot(pick_col.astype(BF16), cos_v[...], preferred_element_type=F32)
        lane = lanes((ROWS, 128))
        turned = pltpu.roll(rows, 64, 1)
        left[who, p, :, 0:128] = jnp.where(lane < 64, rows, turned).astype(BF16)
        left[who, p, :, 128:256] = jnp.where(lane < 64, turned, rows).astype(BF16)
        odd = lax.rem(lax.broadcasted_iota(jnp.int32, (ROWS, 128), 0) // KEEP, 2)
        both = cols + pltpu.roll(cols, 64, 1)
        right[who, p] = jnp.where(lane // 64 == odd, both, 0.0)
        if transposed:
            for q in range(SPANS // 2):
                flat = rows[64 * q:64 * q + 64].T
                high, low = flat[0:64].astype(BF16), flat[64:128].astype(BF16)
                left_t[p, q] = jnp.concatenate([high, high, low, low], axis=1)

    def coefficients(field, who, p):
        found = []
        for h in range(2):
            high, low = split(field[:, 256 * h:256 * h + 256])
            spread = jnp.concatenate([high, low, high, low], axis=0)
            t = jnp.dot(left[who, p, 128 * h:128 * h + 128, :], spread, preferred_element_type=F32)
            t = jnp.concatenate([t[0:64, 0:128], t[64:128, 128:256]], axis=0)
            found.append(jnp.sum(t * right[who, p, 128 * h:128 * h + 128, :], axis=1, keepdims=True))
        return jnp.concatenate(found, axis=0)

    raw_copy(ACROSS, 0).wait()

    @pl.loop(0, HALF)
    def _(i):
        for way in range(2):
            k, p = source(0, way, i)
            add_sibling(k, p)
            y_copy(0, way, i, part.at[k, p]).start()

    for k in order[1:]:
        raw_copy(k, 0).wait()

    @pl.loop(0, EARLY)
    def _(i):
        for way in range(2):
            k, p = source(1, way, i)
            add_sibling(k, p)
            y_copy(1, way, i, part.at[k, p]).start()

    cos_copy.wait()
    for way in range(2):
        p_copy(way).wait_recv()

    for who in (1, 2):
        @pl.loop(0, PIECES, unroll=4)
        def _(p):
            prepare(who, p, False)

    @pl.loop(EARLY, HALF)
    def _(i):
        for way in range(2):
            add_sibling(*source(1, way, i))

    csend[...] = jnp.zeros((2, TILES, 8, 128), F32)

    def add_coefficients(way, k, p):
        csend[way, p // 4] += pack(coefficients(part[k, p], (1, 2)[way], p), p)

    @pl.loop(0, HALF)
    def _(i):
        for way in range(2):
            add_coefficients(way, *source(1, way, i))

    @pl.loop(0, HALF)
    def _(i):
        for way in range(2):
            add_sibling(*source(2, way, i))

    mom_copy.wait()

    @pl.loop(0, PIECES)
    def _(p):
        x_copy(0, p).wait_recv()
        summed = part[0, p] + raw_v[0, 0, :, columns(p)].astype(F32)
        base[p] = 0.999 * mom_v[:, columns(p)] + summed * 0.125

    @pl.loop(0, PIECES, unroll=2)
    def _(p):
        prepare(0, p, True)

    @pl.loop(0, HALF)
    def _(i):
        for way in range(2):
            k, p = source(2, way, i)
            y_copy(0, way, i, ya.at[way, i]).wait_recv()
            part[k, p] = part[k, p] + ya[way, i]
        for way in range(2):
            add_coefficients(way, *source(2, way, i))

    def c_copy(way):
        return pltpu.make_async_remote_copy(
            csend.at[way], crecv.at[way], c_send_sem.at[way], c_recv_sem.at[way],
            device_id=y_peer((BEHIND, AHEAD)[way]), device_id_type=MESH)

    for way in range(2):
        c_copy(way).start()

    @pl.loop(EARLY, HALF)
    def _(i):
        for way in range(2):
            k, p = source(1, way, i)
            y_copy(1, way, i, part.at[k, p]).start()

    @pl.loop(0, HALF)
    def _(i):
        for way in range(2):
            k, p = source(2, way, i)
            y_copy(2, way, i, part.at[k, p]).start()

    xslots[x, core] = jnp.zeros((TILES, 8, 128), F32)

    @pl.loop(0, PIECES, unroll=2)
    def _(p):
        xslots[x, core, p // 4] += pack(coefficients(base[p], 0, p), p)

    for way in range(2):
        c_copy(way).wait_recv()
    xslots[x, core] = xslots[x, core] + (crecv[0] + crecv[1]) * 0.125

    def pair_copy(back):
        ref = total.at[1] if back else xslots.at[x, 1]
        return pltpu.make_async_remote_copy(
            ref, ref, pair_send_sem.at[back], pair_recv_sem.at[back],
            device_id=sibling, device_id_type=MESH)

    def rx_copy(step):
        return pltpu.make_async_remote_copy(
            xslots.at[x], xslots.at[x], rx_send_sem.at[step - 1], rx_recv_sem.at[step - 1],
            device_id=x_peer(step), device_id_type=MESH)

    def rz_copy(step):
        return pltpu.make_async_remote_copy(
            zslots.at[z], zslots.at[z], rz_send_sem.at[step - 1], rz_recv_sem.at[step - 1],
            device_id=z_peer(step), device_id_type=MESH)

    @pl.when(core == 1)
    def _():
        pair_copy(0).start()

    @pl.when(core == 0)
    def _():
        pl.semaphore_wait(barrier, X - 1 + Z - 1)
        pair_copy(0).wait_recv()
        for step in range(1, X):
            rx_copy(step).start()

    def inverse(p, q, column):
        high, low = split(column * right[0, p, 64 * q:64 * q + 64, :])
        spread = jnp.concatenate([high, low, high, low], axis=0)
        return jnp.dot(left_t[p, q], spread, preferred_element_type=F32)

    @pl.loop(0, PIECES, unroll=4)
    def _(p):
        column = unpack(xslots[x, core, p // 4], p)
        for q in range(SPANS // 2):
            base[p, :, 128 * q:128 * q + 128] -= inverse(p, q, column[64 * q:64 * q + 64])

    @pl.when(core == 0)
    def _():
        for step in range(1, X):
            rx_copy(step).wait_recv()
        zslots[z] = (xslots[0] + xslots[1]) + (xslots[2] + xslots[3])
        for step in range(1, Z):
            rz_copy(step).start()
        for step in range(1, Z):
            rz_copy(step).wait_recv()
        summed = zslots[0]
        for s in range(1, Z):
            summed = summed + zslots[s]
        total[...] = summed
        pair_copy(1).start()

    @pl.when(core == 1)
    def _():
        pair_copy(1).wait_recv()

    @pl.loop(0, PIECES, unroll=4)
    def _(p):
        column = unpack(total[core, p // 4], p)
        mean = jnp.sum((column * column).reshape(SPANS, KEEP, 1), axis=1, keepdims=True)
        scale = 1.0 / jnp.sqrt(mean * (1.0 / (BLOCK * BLOCK)) + 1e-06)
        column = column * jnp.broadcast_to(scale, (SPANS, KEEP, 1)).reshape(ROWS, 1)
        for q in range(SPANS // 2):
            at = pl.ds(pl.multiple_of(p * COLS + 128 * q, 128), 128)
            out_u[:, at] = jnp.tanh(inverse(p, q, column[64 * q:64 * q + 64]))

    @pl.loop(0, HALF)
    def _(i):
        for way in range(2):
            p = (HALF + i, i)[way]
            y_copy(1, way, i, yb.at[way, i]).wait_recv()
            base[p] += yb[way, i] * 0.125

    @pl.loop(0, HALF)
    def _(i):
        for way in range(2):
            p = (i, HALF + i)[way]
            y_copy(2, way, i, yc.at[way, i]).wait_recv()
            out_m[0, :, columns(p)] = base[p] + yc[way, i] * 0.125

    for way in range(2):
        p_copy(way).wait_send()
        c_copy(way).wait_send()

    @pl.when(core == 1)
    def _():
        pair_copy(0).wait_send()

    @pl.when(core == 0)
    def _():
        pair_copy(1).wait_send()
        for step in range(1, X):
            rx_copy(step).wait_send()
        for step in range(1, Z):
            rz_copy(step).wait_send()

    @pl.loop(0, PIECES)
    def _(p):
        for k in range(Y):
            x_copy(k, p).wait_send()

    @pl.loop(0, HALF)
    def _(i):
        for stage in range(3):
            for way in range(2):
                y_copy(stage, way, i, ya.at[way, i]).wait_send()


def write_out(new_m, new_u, out_m, out_u, sem):
    copy_m = pltpu.make_async_copy(new_m, out_m, sem.at[0])
    copy_u = pltpu.make_async_copy(new_u, out_u, sem.at[1])
    copy_m.start()
    copy_u.start()
    copy_m.wait()
    copy_u.wait()


def per_device(raw_grads, momentum, positions):
    piece = (BLOCK, COLS)
    tiles = (TILES, 8, 128)
    dma = pltpu.SemaphoreType.DMA
    shapes = ((1, BLOCK, WIDTH), (BLOCK, WIDTH))
    anywhere = pl.BlockSpec(memory_space=pl.ANY)
    inputs = (raw_grads, momentum, positions.T, jnp.asarray(dct_tables()))
    results = pl.pallas_call(
        kernel,
        out_shape=tuple(pltpu.VMEM(shape, F32) for shape in shapes),
        in_specs=[anywhere] * 4,
        out_specs=tuple(pl.BlockSpec(memory_space=pltpu.VMEM) for _ in shapes),
        scratch_shapes=[
            pltpu.VMEM((Y, 2, BLOCK, WIDTH), BF16),
            pltpu.VMEM((BLOCK, WIDTH), F32),
            pltpu.VMEM((KEEP, WIDTH // BLOCK), jnp.int32),
            pltpu.VMEM((BLOCK, 2 * BLOCK), BF16),
            pltpu.VMEM((Y, PIECES) + piece, F32),
            pltpu.VMEM((Y, PIECES) + piece, F32),
            pltpu.VMEM((2, HALF) + piece, F32),
            pltpu.VMEM((2, HALF) + piece, F32),
            pltpu.VMEM((2, HALF) + piece, F32),
            pltpu.VMEM((PIECES,) + piece, F32),
            pltpu.VMEM((3,) + tiles, F32),
            pltpu.VMEM((3, PIECES, ROWS, 256), BF16),
            pltpu.VMEM((3, PIECES, ROWS, 128), F32),
            pltpu.VMEM((PIECES, SPANS // 2, BLOCK, 256), BF16),
            pltpu.VMEM((2,) + tiles, F32),
            pltpu.VMEM((2,) + tiles, F32),
            pltpu.VMEM((X, CORES) + tiles, F32),
            pltpu.VMEM((Z, CORES) + tiles, F32),
            pltpu.VMEM((CORES,) + tiles, F32),
            dma((Y, 2)), dma((3,)), pltpu.SemaphoreType.REGULAR,
            dma((Y, PIECES)), dma((Y, PIECES)),
            dma((3, 2, HALF)), dma((3, 2, HALF)),
            dma((2,)), dma((2,)), dma((2,)), dma((2,)),
            dma((X - 1,)), dma((X - 1,)), dma((Z - 1,)), dma((Z - 1,)),
            dma((2,)), dma((2,)),
        ],
        compiler_params=pltpu.CompilerParams(
            collective_id=0, has_side_effects=True, vmem_limit_bytes=48 * 1024 * 1024),
    )(*(pltpu.with_memory_space_constraint(v, pltpu.HBM) for v in inputs))
    return pl.pallas_call(
        write_out,
        out_shape=tuple(pltpu.HBM(shape, F32) for shape in shapes),
        in_specs=[anywhere] * 2,
        out_specs=(anywhere, anywhere),
        scratch_shapes=[dma((2,))],
        compiler_params=pltpu.CompilerParams(vmem_limit_bytes=4 * 1024 * 1024),
    )(*(pltpu.with_memory_space_constraint(v, pltpu.VMEM) for v in results))


def solution(mesh):
    placed = (P(("rep", "fsdp"), None, None), P("rep", None, "fsdp"), P("fsdp", None))
    return jax.shard_map(
        per_device,
        mesh=mesh,
        in_specs=placed,
        out_specs=(P("rep", None, "fsdp"), P(None, "fsdp")),
        check_vma=False,
    )
```

time: 72.1 us -> 46.5 us (0.64)
  the two profiles are of different devices: /device:TPU:8 before, /device:TPU:1 now
where the time goes in v2:
time: 46.5 us; the launch traced here: 46.4 us
  Pallas kernels  45.8 us (98%)
  between operations  0.64 us (1%)
    pallas_call x1, Pallas kernels, per_device(): pl.pallas_call(kernel, out_shape=tuple((pltpu.VMEM(shape, F32) for shape...  44.5 us
    pallas_call x1, Pallas kernels, per_device(): pl.pallas_call(write_out, out_shape=tuple((pltpu.HBM(shape, F32) for shap...  1.33 us

profile of v2, /device:TPU:1, one launch (start us, length us, event | category | flops | bytes accessed | tf_op | source)
XLA Modules:
  0.0 46.4 jit_solution(15970337491809991235)
XLA Ops:
  0.6 44.5 %shard_map.59 = (f32[1,64,4096]{2,1,0:T(8,128)S(1)}, f32[64,4096]{1,0:T(8,128)S(1)}) custom-call(bf16[1,64,32768]{2,1,0:T(8,128)(2,1)} %raw.1, f32[1,64,4096]{2,1,0:T(8,128)} %mom.1, s32[32,64]{1,0:T(8,128)} %bitcast.1, bf16[64,128]{1,0:T(8,128)(2,1)} %constant.2.clone.cos), custom_call_target="tpu_custom_call" | custom-call | tf_op jit(solution)/shard_map/pallas_call | solution.py:446
  45.1 1.3 %shard_map.60 = (f32[1,64,4096]{2,1,0:T(8,128)}, f32[64,4096]{1,0:T(8,128)}) custom-call(f32[1,64,4096]{2,1,0:T(8,128)S(1)} %get-tuple-element.4.new_m, f32[64,4096]{1,0:T(8,128)S(1)} %get-tuple-element.5.new_u), custom_call_target="tpu_custom_call" | custom-call | tf_op jit(solution)/shard_map/pallas_call | solution.py:481

commit v3 on v2

--- a/solution.py
+++ b/solution.py
@@ -23,7 +23,8 @@
 ROWS = SPANS * KEEP
 TILES = PIECES * SPANS * KEEP // (8 * 128)
 AHEAD, BEHIND, ACROSS = 1, 3, 2
-EARLY = 2
+X_STEPS, Z_STEPS = (2, 1, 3), (4, 3, 5, 2, 6, 1, 7)
+EARLY = 1
 
 
 def dct_tables():
@@ -94,10 +95,6 @@
     @pl.when(core == 0)
     def _():
         greet(sibling)
-        for step in range(1, X):
-            greet(x_peer(step))
-        for step in range(1, Z):
-            greet(z_peer(step))
 
     def raw_copy(k, slot):
         owner = lax.rem(y + k, Y) * CORES + (core if slot == 0 else 1 - core)
@@ -106,17 +103,12 @@
             raw.at[0, :, pl.ds(start, WIDTH)], raw_v.at[k, slot], raw_sem.at[k, slot])
 
     order = (ACROSS, BEHIND, AHEAD, 0)
-    raw_copy(ACROSS, 1).start()
-    raw_copy(ACROSS, 0).start()
     pos_copy = pltpu.make_async_copy(pos, pos_v, in_sem.at[0])
     cos_copy = pltpu.make_async_copy(cos, cos_v, in_sem.at[1])
     mom_copy = pltpu.make_async_copy(mom.at[0], mom_v, in_sem.at[2])
+    raw_copy(ACROSS, 1).start()
     pos_copy.start()
-    cos_copy.start()
-    for k in order[1:]:
-        raw_copy(k, 1).start()
-        raw_copy(k, 0).start()
-    mom_copy.start()
+    raw_copy(ACROSS, 0).start()
 
     def columns(piece):
         return pl.ds(pl.multiple_of(piece * COLS, COLS), COLS)
@@ -128,26 +120,6 @@
 
     def widen(k, p):
         xsend[k, p] = raw_v[k, 1, :, columns(p)].astype(F32)
-
-    raw_copy(ACROSS, 1).wait()
-
-    @pl.loop(0, PIECES)
-    def _(p):
-        widen(ACROSS, p)
-
-    @pl.when(core == 1)
-    def _():
-        pl.semaphore_wait(barrier, 5)
-        pl.semaphore_signal(go_sem, inc=1, device_id=sibling, device_id_type=MESH)
-
-    @pl.when(core == 0)
-    def _():
-        pl.semaphore_wait(go_sem, 1)
-
-    @pl.loop(0, HALF)
-    def _(i):
-        x_copy(ACROSS, i).start()
-        x_copy(ACROSS, HALF + i).start()
 
     pos_copy.wait()
     found = pos_v[...].astype(F32).T
@@ -160,17 +132,36 @@
             places.at[0], places.at[1 + way], p_send_sem.at[way], p_recv_sem.at[way],
             device_id=y_peer((AHEAD, BEHIND)[way]), device_id_type=MESH)
 
+    raw_copy(ACROSS, 1).wait()
+
+    @pl.loop(0, PIECES)
+    def _(p):
+        widen(ACROSS, p)
+
+    @pl.when(core == 1)
+    def _():
+        pl.semaphore_wait(barrier, 5)
+        pl.semaphore_signal(go_sem, inc=1, device_id=sibling, device_id_type=MESH)
+
+    @pl.when(core == 0)
+    def _():
+        pl.semaphore_wait(go_sem, 1)
+
+    x_copy(ACROSS, 0).start()
+    x_copy(ACROSS, HALF).start()
     for way in range(2):
         p_copy(way).start()
 
+    @pl.loop(1, HALF)
+    def _(i):
+        x_copy(ACROSS, i).start()
+        x_copy(ACROSS, HALF + i).start()
+
     for k in order[1:]:
-        raw_copy(k, 1).wait()
-
-        @pl.loop(0, HALF)
-        def _(i):
-            for p in (i, HALF + i):
-                widen(k, p)
-                x_copy(k, p).start()
+        raw_copy(k, 1).start()
+        raw_copy(k, 0).start()
+    cos_copy.start()
+    mom_copy.start()
 
     def y_copy(stage, way, i, src):
         dst = (ya, yb, yc)[stage]
@@ -229,6 +220,22 @@
             y_copy(0, way, i, part.at[k, p]).start()
 
     for k in order[1:]:
+        raw_copy(k, 1).wait()
+
+        @pl.loop(0, HALF)
+        def _(i):
+            for p in (i, HALF + i):
+                widen(k, p)
+                x_copy(k, p).start()
+
+    @pl.when(core == 0)
+    def _():
+        for step in range(1, X):
+            greet(x_peer(step))
+        for step in range(1, Z):
+            greet(z_peer(step))
+
+    for k in order[1:]:
         raw_copy(k, 0).wait()
 
     @pl.loop(0, EARLY)
@@ -296,17 +303,20 @@
     for way in range(2):
         c_copy(way).start()
 
-    @pl.loop(EARLY, HALF)
-    def _(i):
-        for way in range(2):
-            k, p = source(1, way, i)
-            y_copy(1, way, i, part.at[k, p]).start()
-
-    @pl.loop(0, HALF)
-    def _(i):
-        for way in range(2):
-            k, p = source(2, way, i)
-            y_copy(2, way, i, part.at[k, p]).start()
+    def send_rest():
+        @pl.loop(EARLY, HALF)
+        def _(i):
+            for way in range(2):
+                k, p = source(1, way, i)
+                y_copy(1, way, i, part.at[k, p]).start()
+
+        @pl.loop(0, HALF)
+        def _(i):
+            for way in range(2):
+                k, p = source(2, way, i)
+                y_copy(2, way, i, part.at[k, p]).start()
+
+    pl.when(core == 1)(send_rest)
 
     xslots[x, core] = jnp.zeros((TILES, 8, 128), F32)
 
@@ -342,7 +352,7 @@
     def _():
         pl.semaphore_wait(barrier, X - 1 + Z - 1)
         pair_copy(0).wait_recv()
-        for step in range(1, X):
+        for step in X_STEPS:
             rx_copy(step).start()
 
     def inverse(p, q, column):
@@ -360,8 +370,9 @@
     def _():
         for step in range(1, X):
             rx_copy(step).wait_recv()
+        send_rest()
         zslots[z] = (xslots[0] + xslots[1]) + (xslots[2] + xslots[3])
-        for step in range(1, Z):
+        for step in Z_STEPS:
             rz_copy(step).start()
         for step in range(1, Z):
             rz_copy(step).wait_recv()
@@ -392,13 +403,6 @@
             y_copy(1, way, i, yb.at[way, i]).wait_recv()
             base[p] += yb[way, i] * 0.125
 
-    @pl.loop(0, HALF)
-    def _(i):
-        for way in range(2):
-            p = (i, HALF + i)[way]
-            y_copy(2, way, i, yc.at[way, i]).wait_recv()
-            out_m[0, :, columns(p)] = base[p] + yc[way, i] * 0.125
-
     for way in range(2):
         p_copy(way).wait_send()
         c_copy(way).wait_send()
@@ -422,9 +426,18 @@
 
     @pl.loop(0, HALF)
     def _(i):
-        for stage in range(3):
+        for stage in range(2):
             for way in range(2):
                 y_copy(stage, way, i, ya.at[way, i]).wait_send()
+
+    @pl.loop(0, HALF)
+    def _(i):
+        for way in range(2):
+            p = (i, HALF + i)[way]
+            y_copy(2, way, i, yc.at[way, i]).wait_recv()
+            out_m[0, :, columns(p)] = base[p] + yc[way, i] * 0.125
+        for way in range(2):
+            y_copy(2, way, i, yc.at[way, i]).wait_send()
 
 
 def write_out(new_m, new_u, out_m, out_u, sem):

time: 46.5 us -> 44.5 us (0.957)
  the two profiles are of different devices: /device:TPU:1 before, /device:TPU:8 now
where the time goes in v3:
time: 44.5 us; the launch traced here: 43.7 us
  Pallas kernels  43.1 us (97%)
  between operations  0.64 us (1%)
    pallas_call x1, Pallas kernels, per_device(): pl.pallas_call(kernel, out_shape=tuple((pltpu.VMEM(shape, F32) for shape...  41.8 us
    pallas_call x1, Pallas kernels, per_device(): pl.pallas_call(write_out, out_shape=tuple((pltpu.HBM(shape, F32) for shap...  1.33 us

profile of v3, /device:TPU:8, one launch (start us, length us, event | category | flops | bytes accessed | tf_op | source)
XLA Modules:
  0.0 43.7 jit_solution(16080893215578483197)
XLA Ops:
  0.6 41.8 %shard_map.59 = (f32[1,64,4096]{2,1,0:T(8,128)S(1)}, f32[64,4096]{1,0:T(8,128)S(1)}) custom-call(bf16[1,64,32768]{2,1,0:T(8,128)(2,1)} %raw.1, f32[1,64,4096]{2,1,0:T(8,128)} %mom.1, s32[32,64]{1,0:T(8,128)} %bitcast.1, bf16[64,128]{1,0:T(8,128)(2,1)} %constant.2.clone.cos), custom_call_target="tpu_custom_call" | custom-call | tf_op jit(solution)/shard_map/pallas_call | solution.py:459
  42.4 1.3 %shard_map.60 = (f32[1,64,4096]{2,1,0:T(8,128)}, f32[64,4096]{1,0:T(8,128)}) custom-call(f32[1,64,4096]{2,1,0:T(8,128)S(1)} %get-tuple-element.4.new_m, f32[64,4096]{1,0:T(8,128)S(1)} %get-tuple-element.5.new_u), custom_call_target="tpu_custom_call" | custom-call | tf_op jit(solution)/shard_map/pallas_call | solution.py:494

commit v4 on v3

--- a/solution.py
+++ b/solution.py
@@ -65,7 +65,7 @@
     raw, mom, pos, cos, out_m, out_u,
     raw_v, mom_v, pos_v, cos_v, xsend, part, ya, yb, yc, base,
     places, left, right, left_t, csend, crecv, xslots, zslots, total,
-    raw_sem, in_sem, go_sem, x_send_sem, x_recv_sem, y_send_sem, y_recv_sem,
+    raw_sem, in_sem, go_sem, near_sem, x_send_sem, x_recv_sem, y_send_sem, y_recv_sem,
     p_send_sem, p_recv_sem, c_send_sem, c_recv_sem,
     rx_send_sem, rx_recv_sem, rz_send_sem, rz_recv_sem, pair_send_sem, pair_recv_sem,
 ):
@@ -85,12 +85,15 @@
     sibling = (rep, y * CORES + 1 - core)
 
     barrier = pltpu.get_barrier_semaphore()
+    odd = lax.rem(y, 2) == 1
 
     def greet(peer):
         pl.semaphore_signal(barrier, inc=1, device_id=peer, device_id_type=MESH)
 
-    greet(y_peer(AHEAD, 1))
-    greet(y_peer(BEHIND, 1))
+    @pl.when(jnp.logical_not(odd))
+    def _():
+        greet(y_peer(AHEAD, 1))
+        greet(y_peer(BEHIND, 1))
 
     @pl.when(core == 0)
     def _():
@@ -138,21 +141,29 @@
     def _(p):
         widen(ACROSS, p)
 
+    def tell(sem, peer):
+        pl.semaphore_signal(sem, inc=1, device_id=peer, device_id_type=MESH)
+
     @pl.when(core == 1)
     def _():
-        pl.semaphore_wait(barrier, 5)
-        pl.semaphore_signal(go_sem, inc=1, device_id=sibling, device_id_type=MESH)
+        @pl.when(odd)
+        def _():
+            pl.semaphore_wait(barrier, 5)
+            for step in (AHEAD, BEHIND):
+                for of in range(CORES):
+                    tell(near_sem, y_peer(step, of))
+
+        @pl.when(jnp.logical_not(odd))
+        def _():
+            pl.semaphore_wait(barrier, 1)
+
+        tell(go_sem, sibling)
 
     @pl.when(core == 0)
     def _():
         pl.semaphore_wait(go_sem, 1)
 
-    x_copy(ACROSS, 0).start()
-    x_copy(ACROSS, HALF).start()
-    for way in range(2):
-        p_copy(way).start()
-
-    @pl.loop(1, HALF)
+    @pl.loop(0, HALF)
     def _(i):
         x_copy(ACROSS, i).start()
         x_copy(ACROSS, HALF + i).start()
@@ -162,6 +173,13 @@
         raw_copy(k, 0).start()
     cos_copy.start()
     mom_copy.start()
+
+    @pl.when(jnp.logical_not(odd))
+    def _():
+        pl.semaphore_wait(near_sem, 2)
+
+    for way in range(2):
+        p_copy(way).start()
 
     def y_copy(stage, way, i, src):
         dst = (ya, yb, yc)[stage]
@@ -481,7 +499,7 @@
             pltpu.VMEM((X, CORES) + tiles, F32),
             pltpu.VMEM((Z, CORES) + tiles, F32),
             pltpu.VMEM((CORES,) + tiles, F32),
-            dma((Y, 2)), dma((3,)), pltpu.SemaphoreType.REGULAR,
+            dma((Y, 2)), dma((3,)), pltpu.SemaphoreType.REGULAR, pltpu.SemaphoreType.REGULAR,
             dma((Y, PIECES)), dma((Y, PIECES)),
             dma((3, 2, HALF)), dma((3, 2, HALF)),
             dma((2,)), dma((2,)), dma((2,)), dma((2,)),

time: 44.5 us -> 44.1 us (level)
  no operation moved by 1% of the time
where the time goes in v4:
time: 44.1 us; the launch traced here: 43.8 us
  Pallas kernels  43.1 us (98%)
  between operations  0.64 us (1%)
    pallas_call x1, Pallas kernels, per_device(): pl.pallas_call(kernel, out_shape=tuple((pltpu.VMEM(shape, F32) for shape...  41.8 us
    pallas_call x1, Pallas kernels, per_device(): pl.pallas_call(write_out, out_shape=tuple((pltpu.HBM(shape, F32) for shap...  1.33 us

profile of v4, /device:TPU:8, one launch (start us, length us, event | category | flops | bytes accessed | tf_op | source)
XLA Modules:
  0.0 43.8 jit_solution(10771099488644110656)
XLA Ops:
  0.6 41.8 %shard_map.59 = (f32[1,64,4096]{2,1,0:T(8,128)S(1)}, f32[64,4096]{1,0:T(8,128)S(1)}) custom-call(bf16[1,64,32768]{2,1,0:T(8,128)(2,1)} %raw.1, f32[1,64,4096]{2,1,0:T(8,128)} %mom.1, s32[32,64]{1,0:T(8,128)} %bitcast.1, bf16[64,128]{1,0:T(8,128)(2,1)} %constant.2.clone.cos), custom_call_target="tpu_custom_call" | custom-call | tf_op jit(solution)/shard_map/pallas_call | solution.py:477
  42.4 1.3 %shard_map.60 = (f32[1,64,4096]{2,1,0:T(8,128)}, f32[64,4096]{1,0:T(8,128)}) custom-call(f32[1,64,4096]{2,1,0:T(8,128)S(1)} %get-tuple-element.4.new_m, f32[64,4096]{1,0:T(8,128)S(1)} %get-tuple-element.5.new_u), custom_call_target="tpu_custom_call" | custom-call | tf_op jit(solution)/shard_map/pallas_call | solution.py:512

commit v5 on v4

--- a/solution.py
+++ b/solution.py
@@ -18,6 +18,7 @@
 WIDTH = 4096
 PIECES = 8
 HALF = PIECES // 2
+LAST = HALF - 1
 COLS = WIDTH // PIECES
 SPANS = COLS // BLOCK
 ROWS = SPANS * KEEP
@@ -63,9 +64,9 @@
 
 def kernel(
     raw, mom, pos, cos, out_m, out_u,
-    raw_v, mom_v, pos_v, cos_v, xsend, part, ya, yb, yc, base,
+    raw_v, mom_v, pos_v, cos_v, xsend, part, ya, yh, yb, yc, base,
     places, left, right, left_t, csend, crecv, xslots, zslots, total,
-    raw_sem, in_sem, go_sem, near_sem, x_send_sem, x_recv_sem, y_send_sem, y_recv_sem,
+    raw_sem, in_sem, go_sem, near_sem, x_send_sem, x_recv_sem, y_send_sem, y_recv_sem, h_send_sem, h_recv_sem,
     p_send_sem, p_recv_sem, c_send_sem, c_recv_sem,
     rx_send_sem, rx_recv_sem, rz_send_sem, rz_recv_sem, pair_send_sem, pair_recv_sem,
 ):
@@ -124,23 +125,6 @@
     def widen(k, p):
         xsend[k, p] = raw_v[k, 1, :, columns(p)].astype(F32)
 
-    pos_copy.wait()
-    found = pos_v[...].astype(F32).T
-    for m in range(TILES):
-        places[0, m] = jnp.concatenate(
-            [found[8 * (4 * m + j):8 * (4 * m + j) + 8] for j in range(4)], axis=1)
-
-    def p_copy(way):
-        return pltpu.make_async_remote_copy(
-            places.at[0], places.at[1 + way], p_send_sem.at[way], p_recv_sem.at[way],
-            device_id=y_peer((AHEAD, BEHIND)[way]), device_id_type=MESH)
-
-    raw_copy(ACROSS, 1).wait()
-
-    @pl.loop(0, PIECES)
-    def _(p):
-        widen(ACROSS, p)
-
     def tell(sem, peer):
         pl.semaphore_signal(sem, inc=1, device_id=peer, device_id_type=MESH)
 
@@ -163,10 +147,13 @@
     def _():
         pl.semaphore_wait(go_sem, 1)
 
+    raw_copy(ACROSS, 1).wait()
+
     @pl.loop(0, HALF)
     def _(i):
-        x_copy(ACROSS, i).start()
-        x_copy(ACROSS, HALF + i).start()
+        for p in (i, PIECES - 1 - i):
+            widen(ACROSS, p)
+            x_copy(ACROSS, p).start()
 
     for k in order[1:]:
         raw_copy(k, 1).start()
@@ -174,6 +161,17 @@
     cos_copy.start()
     mom_copy.start()
 
+    pos_copy.wait()
+    found = pos_v[...].astype(F32).T
+    for m in range(TILES):
+        places[0, m] = jnp.concatenate(
+            [found[8 * (4 * m + j):8 * (4 * m + j) + 8] for j in range(4)], axis=1)
+
+    def p_copy(way):
+        return pltpu.make_async_remote_copy(
+            places.at[0], places.at[1 + way], p_send_sem.at[way], p_recv_sem.at[way],
+            device_id=y_peer((AHEAD, BEHIND)[way]), device_id_type=MESH)
+
     @pl.when(jnp.logical_not(odd))
     def _():
         pl.semaphore_wait(near_sem, 2)
@@ -192,11 +190,12 @@
         part[k, p] = part[k, p] + raw_v[k, 0, :, columns(p)].astype(F32)
 
     def source(stage, way, i):
+        low, high = i, PIECES - 1 - i
         if stage == 0:
-            return ACROSS, (i, HALF + i)[way]
+            return ACROSS, (low, high)[way]
         if stage == 1:
-            return (BEHIND, AHEAD)[way], (HALF + i, i)[way]
-        return (BEHIND, AHEAD)[way], (i, HALF + i)[way]
+            return (BEHIND, AHEAD)[way], (high, low)[way]
+        return (BEHIND, AHEAD)[way], (low, high)[way]
 
     def prepare(who, p, transposed):
         place = unpack(places[who, p // 4], p).astype(jnp.int32)
@@ -230,19 +229,45 @@
 
     raw_copy(ACROSS, 0).wait()
 
-    @pl.loop(0, HALF)
+    shared = jnp.where(y == 1, LAST, HALF)
+    halves = (pl.ds(0, COLS // 2), pl.ds(COLS // 2, COLS // 2))
+    halving = jnp.logical_and(core == 0, lax.rem(y, 2) == 1)
+    halved = jnp.logical_and(core == 0, lax.rem(y, 2) == 0)
+
+    def h_copy(way):
+        return pltpu.make_async_remote_copy(
+            part.at[ACROSS, shared, :, halves[way]], yh.at[way], h_send_sem.at[way], h_recv_sem.at[way],
+            device_id=y_peer((BEHIND, AHEAD)[way]), device_id_type=MESH)
+
+    def whole(way):
+        return jnp.logical_not(jnp.logical_and(core == 0, y == (1, 3)[way]))
+
+    @pl.loop(0, LAST)
     def _(i):
         for way in range(2):
             k, p = source(0, way, i)
             add_sibling(k, p)
             y_copy(0, way, i, part.at[k, p]).start()
 
+    for way in range(2):
+        add_sibling(*source(0, way, LAST))
+
+    for way in range(2):
+        @pl.when(whole(way))
+        def _():
+            y_copy(0, way, LAST, part.at[source(0, way, LAST)]).start()
+
+    @pl.when(halving)
+    def _():
+        for way in range(2):
+            h_copy(way).start()
+
     for k in order[1:]:
         raw_copy(k, 1).wait()
 
         @pl.loop(0, HALF)
         def _(i):
-            for p in (i, HALF + i):
+            for p in (i, PIECES - 1 - i):
                 widen(k, p)
                 x_copy(k, p).start()
 
@@ -282,7 +307,9 @@
     def add_coefficients(way, k, p):
         csend[way, p // 4] += pack(coefficients(part[k, p], (1, 2)[way], p), p)
 
-    @pl.loop(0, HALF)
+    joined = jnp.logical_and(core == 0, y == 2)
+
+    @pl.loop(0, LAST + jnp.where(joined, 0, 1))
     def _(i):
         for way in range(2):
             add_coefficients(way, *source(1, way, i))
@@ -304,14 +331,37 @@
     def _(p):
         prepare(0, p, True)
 
-    @pl.loop(0, HALF)
-    def _(i):
-        for way in range(2):
-            k, p = source(2, way, i)
-            y_copy(0, way, i, ya.at[way, i]).wait_recv()
-            part[k, p] = part[k, p] + ya[way, i]
+    def relay(way, i):
+        k, p = source(2, way, i)
+        y_copy(0, way, i, ya.at[way, i]).wait_recv()
+        part[k, p] = part[k, p] + ya[way, i]
+
+    @pl.loop(0, LAST)
+    def _(i):
+        for way in range(2):
+            relay(way, i)
         for way in range(2):
             add_coefficients(way, *source(2, way, i))
+
+    @pl.when(jnp.logical_not(jnp.logical_and(core == 0, y == 0)))
+    def _():
+        for way in range(2):
+            relay(way, LAST)
+
+    @pl.when(halved)
+    def _():
+        for way in range(2):
+            k, p = (BEHIND, AHEAD)[way], jnp.where(y == (0, 2)[way], LAST, HALF)
+            h_copy(way).wait_recv()
+            part[k, p, :, halves[way]] = part[k, p, :, halves[way]] + yh[way]
+
+    for way in range(2):
+        add_coefficients(way, *source(2, way, LAST))
+
+    @pl.when(joined)
+    def _():
+        for way in range(2):
+            add_coefficients(way, *source(1, way, LAST))
 
     def c_copy(way):
         return pltpu.make_async_remote_copy(
@@ -417,7 +467,7 @@
     @pl.loop(0, HALF)
     def _(i):
         for way in range(2):
-            p = (HALF + i, i)[way]
+            p = (PIECES - 1 - i, i)[way]
             y_copy(1, way, i, yb.at[way, i]).wait_recv()
             base[p] += yb[way, i] * 0.125
 
@@ -442,16 +492,30 @@
         for k in range(Y):
             x_copy(k, p).wait_send()
 
+    @pl.loop(0, LAST)
+    def _(i):
+        for way in range(2):
+            y_copy(0, way, i, ya.at[way, i]).wait_send()
+
+    for way in range(2):
+        @pl.when(whole(way))
+        def _():
+            y_copy(0, way, LAST, ya.at[way, LAST]).wait_send()
+
+    @pl.when(halving)
+    def _():
+        for way in range(2):
+            h_copy(way).wait_send()
+
     @pl.loop(0, HALF)
     def _(i):
-        for stage in range(2):
-            for way in range(2):
-                y_copy(stage, way, i, ya.at[way, i]).wait_send()
+        for way in range(2):
+            y_copy(1, way, i, yb.at[way, i]).wait_send()
 
     @pl.loop(0, HALF)
     def _(i):
         for way in range(2):
-            p = (i, HALF + i)[way]
+            p = (i, PIECES - 1 - i)[way]
             y_copy(2, way, i, yc.at[way, i]).wait_recv()
             out_m[0, :, columns(p)] = base[p] + yc[way, i] * 0.125
         for way in range(2):
@@ -487,6 +551,7 @@
             pltpu.VMEM((Y, PIECES) + piece, F32),
             pltpu.VMEM((Y, PIECES) + piece, F32),
             pltpu.VMEM((2, HALF) + piece, F32),
+            pltpu.VMEM((2, BLOCK, COLS // 2), F32),
             pltpu.VMEM((2, HALF) + piece, F32),
             pltpu.VMEM((2, HALF) + piece, F32),
             pltpu.VMEM((PIECES,) + piece, F32),
@@ -501,7 +566,7 @@
             pltpu.VMEM((CORES,) + tiles, F32),
             dma((Y, 2)), dma((3,)), pltpu.SemaphoreType.REGULAR, pltpu.SemaphoreType.REGULAR,
             dma((Y, PIECES)), dma((Y, PIECES)),
-            dma((3, 2, HALF)), dma((3, 2, HALF)),
+            dma((3, 2, HALF)), dma((3, 2, HALF)), dma((2,)), dma((2,)),
             dma((2,)), dma((2,)), dma((2,)), dma((2,)),
             dma((X - 1,)), dma((X - 1,)), dma((Z - 1,)), dma((Z - 1,)),
             dma((2,)), dma((2,)),

time: 44.1 us -> 43.9 us (level)
  no operation moved by 1% of the time
where the time goes in v5:
time: 43.9 us; the launch traced here: 43.8 us
  Pallas kernels  43.2 us (98%)
  between operations  0.64 us (1%)
    pallas_call x1, Pallas kernels, per_device(): pl.pallas_call(kernel, out_shape=tuple((pltpu.VMEM(shape, F32) for shape...  41.8 us
    pallas_call x1, Pallas kernels, per_device(): pl.pallas_call(write_out, out_shape=tuple((pltpu.HBM(shape, F32) for shap...  1.33 us

profile of v5, /device:TPU:8, one launch (start us, length us, event | category | flops | bytes accessed | tf_op | source)
XLA Modules:
  0.0 43.8 jit_solution(14102330284782207921)
XLA Ops:
  0.6 41.8 %shard_map.59 = (f32[1,64,4096]{2,1,0:T(8,128)S(1)}, f32[64,4096]{1,0:T(8,128)S(1)}) custom-call(bf16[1,64,32768]{2,1,0:T(8,128)(2,1)} %raw.1, f32[1,64,4096]{2,1,0:T(8,128)} %mom.1, s32[32,64]{1,0:T(8,128)} %bitcast.1, bf16[64,128]{1,0:T(8,128)(2,1)} %constant.2.clone.cos), custom_call_target="tpu_custom_call" | custom-call | tf_op jit(solution)/shard_map/pallas_call | solution.py:541
  42.5 1.3 %shard_map.60 = (f32[1,64,4096]{2,1,0:T(8,128)}, f32[64,4096]{1,0:T(8,128)}) custom-call(f32[1,64,4096]{2,1,0:T(8,128)S(1)} %get-tuple-element.4.new_m, f32[64,4096]{1,0:T(8,128)S(1)} %get-tuple-element.5.new_u), custom_call_target="tpu_custom_call" | custom-call | tf_op jit(solution)/shard_map/pallas_call | solution.py:577

commit v6 on v5

--- a/solution.py
+++ b/solution.py
@@ -2,8 +2,6 @@
 
 import jax
 import jax.numpy as jnp
-import ml_dtypes
-import numpy as np
 from jax import lax
 from jax.experimental import pallas as pl
 from jax.experimental.pallas import tpu as pltpu
@@ -28,21 +26,20 @@
 EARLY = 1
 
 
-def dct_tables():
-    k = np.arange(BLOCK)[:, None]
-    j = np.arange(BLOCK)[None, :]
-    cosines = np.cos(np.pi * (j + 0.5) * k / BLOCK) * math.sqrt(2.0 / BLOCK)
-    cosines = np.where(k == 0, cosines * math.sqrt(0.5), cosines)
-    high = cosines.astype(ml_dtypes.bfloat16)
-    low = (cosines - high.astype(np.float64)).astype(ml_dtypes.bfloat16)
-    return np.concatenate([high, low], axis=1)
-
-
 def split(x):
     high = x.astype(BF16)
     return high, (x - high.astype(F32)).astype(BF16)
 
 
+def dct_table():
+    k = lax.broadcasted_iota(jnp.int32, (BLOCK, BLOCK), 0)
+    j = lax.broadcasted_iota(jnp.int32, (BLOCK, BLOCK), 1)
+    turn = lax.rem((2 * j + 1) * k, 4 * BLOCK)
+    cosines = jnp.cos(turn.astype(F32) * (math.pi / (2 * BLOCK))) * math.sqrt(2.0 / BLOCK)
+    high, low = split(jnp.where(k == 0, cosines * math.sqrt(0.5), cosines))
+    return jnp.concatenate([high, low], axis=1)
+
+
 def lanes(shape):
     return lax.broadcasted_iota(jnp.int32, shape, 1)
 
@@ -63,10 +60,10 @@
 
 
 def kernel(
-    raw, mom, pos, cos, out_m, out_u,
+    raw, mom, pos, out_m, out_u,
     raw_v, mom_v, pos_v, cos_v, xsend, part, ya, yh, yb, yc, base,
     places, left, right, left_t, csend, crecv, xslots, zslots, total,
-    raw_sem, in_sem, go_sem, near_sem, x_send_sem, x_recv_sem, y_send_sem, y_recv_sem, h_send_sem, h_recv_sem,
+    raw_sem, in_sem, go_sem, near_sem, x_send_sem, x_recv_sem, y_send_sem, y_recv_sem, w_send_sem, w_recv_sem, h_send_sem, h_recv_sem,
     p_send_sem, p_recv_sem, c_send_sem, c_recv_sem,
     rx_send_sem, rx_recv_sem, rz_send_sem, rz_recv_sem, pair_send_sem, pair_recv_sem,
 ):
@@ -108,8 +105,7 @@
 
     order = (ACROSS, BEHIND, AHEAD, 0)
     pos_copy = pltpu.make_async_copy(pos, pos_v, in_sem.at[0])
-    cos_copy = pltpu.make_async_copy(cos, cos_v, in_sem.at[1])
-    mom_copy = pltpu.make_async_copy(mom.at[0], mom_v, in_sem.at[2])
+    mom_copy = pltpu.make_async_copy(mom.at[0], mom_v, in_sem.at[1])
     raw_copy(ACROSS, 1).start()
     pos_copy.start()
     raw_copy(ACROSS, 0).start()
@@ -120,6 +116,20 @@
     def x_copy(k, p):
         return pltpu.make_async_remote_copy(
             xsend.at[k, p], part.at[k, p], x_send_sem.at[k, p], x_recv_sem.at[k, p],
+            device_id=sibling, device_id_type=MESH)
+
+    def wide_copy(n, way):
+        k, count = (BEHIND, AHEAD)[way], (LAST, LAST, 1)[n]
+        first = ((HALF, 1), (0, HALF + 1), (LAST, HALF))[n][way]
+        return pltpu.make_async_remote_copy(
+            part.at[k, pl.ds(first, count)], (yb, yc, yc)[n].at[way, pl.ds(first % HALF, count)],
+            w_send_sem.at[n, way], w_recv_sem.at[n, way],
+            device_id=y_peer((BEHIND, AHEAD)[way]), device_id_type=MESH)
+
+    def x_half(k, half):
+        pieces = pl.ds(half * HALF, HALF)
+        return pltpu.make_async_remote_copy(
+            xsend.at[k, pieces], part.at[k, pieces], x_send_sem.at[k, half], x_recv_sem.at[k, half],
             device_id=sibling, device_id_type=MESH)
 
     def widen(k, p):
@@ -158,7 +168,6 @@
     for k in order[1:]:
         raw_copy(k, 1).start()
         raw_copy(k, 0).start()
-    cos_copy.start()
     mom_copy.start()
 
     pos_copy.wait()
@@ -179,14 +188,16 @@
     for way in range(2):
         p_copy(way).start()
 
+    def place_of(stage, way, i):
+        return i if way == stage else LAST - i
+
     def y_copy(stage, way, i, src):
-        dst = (ya, yb, yc)[stage]
-        return pltpu.make_async_remote_copy(
-            src, dst.at[way, i], y_send_sem.at[stage, way, i], y_recv_sem.at[stage, way, i],
+        dst = (ya, yb)[stage]
+        return pltpu.make_async_remote_copy(
+            src, dst.at[way, place_of(stage, way, i)], y_send_sem.at[stage, way, i], y_recv_sem.at[stage, way, i],
             device_id=y_peer((BEHIND, AHEAD)[way]), device_id_type=MESH)
 
     def add_sibling(k, p):
-        x_copy(k, p).wait_recv()
         part[k, p] = part[k, p] + raw_v[k, 0, :, columns(p)].astype(F32)
 
     def source(stage, way, i):
@@ -246,10 +257,12 @@
     def _(i):
         for way in range(2):
             k, p = source(0, way, i)
+            x_copy(k, p).wait_recv()
             add_sibling(k, p)
             y_copy(0, way, i, part.at[k, p]).start()
 
     for way in range(2):
+        x_copy(*source(0, way, LAST)).wait_recv()
         add_sibling(*source(0, way, LAST))
 
     for way in range(2):
@@ -264,12 +277,12 @@
 
     for k in order[1:]:
         raw_copy(k, 1).wait()
-
-        @pl.loop(0, HALF)
-        def _(i):
-            for p in (i, PIECES - 1 - i):
+        for half in (1, 0) if k == BEHIND else (0, 1):
+            @pl.loop(half * HALF, half * HALF + HALF)
+            def _(p):
                 widen(k, p)
-                x_copy(k, p).start()
+
+            x_half(k, half).start()
 
     @pl.when(core == 0)
     def _():
@@ -281,6 +294,9 @@
     for k in order[1:]:
         raw_copy(k, 0).wait()
 
+    x_half(BEHIND, 1).wait_recv()
+    x_half(AHEAD, 0).wait_recv()
+
     @pl.loop(0, EARLY)
     def _(i):
         for way in range(2):
@@ -288,7 +304,7 @@
             add_sibling(k, p)
             y_copy(1, way, i, part.at[k, p]).start()
 
-    cos_copy.wait()
+    cos_v[...] = dct_table()
     for way in range(2):
         p_copy(way).wait_recv()
 
@@ -314,16 +330,20 @@
         for way in range(2):
             add_coefficients(way, *source(1, way, i))
 
+    x_half(BEHIND, 0).wait_recv()
+    x_half(AHEAD, 1).wait_recv()
+
     @pl.loop(0, HALF)
     def _(i):
         for way in range(2):
             add_sibling(*source(2, way, i))
 
     mom_copy.wait()
+    for half in range(2):
+        x_half(0, half).wait_recv()
 
     @pl.loop(0, PIECES)
     def _(p):
-        x_copy(0, p).wait_recv()
         summed = part[0, p] + raw_v[0, 0, :, columns(p)].astype(F32)
         base[p] = 0.999 * mom_v[:, columns(p)] + summed * 0.125
 
@@ -334,7 +354,7 @@
     def relay(way, i):
         k, p = source(2, way, i)
         y_copy(0, way, i, ya.at[way, i]).wait_recv()
-        part[k, p] = part[k, p] + ya[way, i]
+        part[k, p] = part[k, p] + ya[way, place_of(0, way, i)]
 
     @pl.loop(0, LAST)
     def _(i):
@@ -372,17 +392,9 @@
         c_copy(way).start()
 
     def send_rest():
-        @pl.loop(EARLY, HALF)
-        def _(i):
+        for n in range(3):
             for way in range(2):
-                k, p = source(1, way, i)
-                y_copy(1, way, i, part.at[k, p]).start()
-
-        @pl.loop(0, HALF)
-        def _(i):
-            for way in range(2):
-                k, p = source(2, way, i)
-                y_copy(2, way, i, part.at[k, p]).start()
+                wide_copy(n, way).start()
 
     pl.when(core == 1)(send_rest)
 
@@ -464,12 +476,14 @@
             at = pl.ds(pl.multiple_of(p * COLS + 128 * q, 128), 128)
             out_u[:, at] = jnp.tanh(inverse(p, q, column[64 * q:64 * q + 64]))
 
+    for way in range(2):
+        y_copy(1, way, 0, yb.at[way, 0]).wait_recv()
+        wide_copy(0, way).wait_recv()
+
     @pl.loop(0, HALF)
     def _(i):
-        for way in range(2):
-            p = (PIECES - 1 - i, i)[way]
-            y_copy(1, way, i, yb.at[way, i]).wait_recv()
-            base[p] += yb[way, i] * 0.125
+        base[HALF + i] += yb[0, i] * 0.125
+        base[i] += yb[1, i] * 0.125
 
     for way in range(2):
         p_copy(way).wait_send()
@@ -489,8 +503,11 @@
 
     @pl.loop(0, PIECES)
     def _(p):
-        for k in range(Y):
-            x_copy(k, p).wait_send()
+        x_copy(ACROSS, p).wait_send()
+
+    for k in order[1:]:
+        for half in range(2):
+            x_half(k, half).wait_send()
 
     @pl.loop(0, LAST)
     def _(i):
@@ -507,19 +524,27 @@
         for way in range(2):
             h_copy(way).wait_send()
 
-    @pl.loop(0, HALF)
-    def _(i):
-        for way in range(2):
-            y_copy(1, way, i, yb.at[way, i]).wait_send()
-
-    @pl.loop(0, HALF)
-    def _(i):
-        for way in range(2):
-            p = (i, PIECES - 1 - i)[way]
-            y_copy(2, way, i, yc.at[way, i]).wait_recv()
-            out_m[0, :, columns(p)] = base[p] + yc[way, i] * 0.125
-        for way in range(2):
-            y_copy(2, way, i, yc.at[way, i]).wait_send()
+    for way in range(2):
+        y_copy(1, way, 0, yb.at[way, 0]).wait_send()
+        wide_copy(0, way).wait_send()
+
+    def finish(p, way):
+        out_m[0, :, columns(p)] = base[p] + yc[way, lax.rem(p, HALF)] * 0.125
+
+    for way in range(2):
+        wide_copy(1, way).wait_recv()
+
+    @pl.loop(0, LAST)
+    def _(i):
+        finish(i, 0)
+        finish(HALF + 1 + i, 1)
+
+    for way in range(2):
+        wide_copy(2, way).wait_recv()
+        finish(jnp.int32((LAST, HALF)[way]), way)
+    for n in (1, 2):
+        for way in range(2):
+            wide_copy(n, way).wait_send()
 
 
 def write_out(new_m, new_u, out_m, out_u, sem):
@@ -537,11 +562,11 @@
     dma = pltpu.SemaphoreType.DMA
     shapes = ((1, BLOCK, WIDTH), (BLOCK, WIDTH))
     anywhere = pl.BlockSpec(memory_space=pl.ANY)
-    inputs = (raw_grads, momentum, positions.T, jnp.asarray(dct_tables()))
+    inputs = (raw_grads, momentum, positions.T)
     results = pl.pallas_call(
         kernel,
         out_shape=tuple(pltpu.VMEM(shape, F32) for shape in shapes),
-        in_specs=[anywhere] * 4,
+        in_specs=[anywhere] * 3,
         out_specs=tuple(pl.BlockSpec(memory_space=pltpu.VMEM) for _ in shapes),
         scratch_shapes=[
             pltpu.VMEM((Y, 2, BLOCK, WIDTH), BF16),
@@ -564,9 +589,9 @@
             pltpu.VMEM((X, CORES) + tiles, F32),
             pltpu.VMEM((Z, CORES) + tiles, F32),
             pltpu.VMEM((CORES,) + tiles, F32),
-            dma((Y, 2)), dma((3,)), pltpu.SemaphoreType.REGULAR, pltpu.SemaphoreType.REGULAR,
+            dma((Y, 2)), dma((2,)), pltpu.SemaphoreType.REGULAR, pltpu.SemaphoreType.REGULAR,
             dma((Y, PIECES)), dma((Y, PIECES)),
-            dma((3, 2, HALF)), dma((3, 2, HALF)), dma((2,)), dma((2,)),
+            dma((2, 2, HALF)), dma((2, 2, HALF)), dma((3, 2)), dma((3, 2)), dma((2,)), dma((2,)),
             dma((2,)), dma((2,)), dma((2,)), dma((2,)),
             dma((X - 1,)), dma((X - 1,)), dma((Z - 1,)), dma((Z - 1,)),
             dma((2,)), dma((2,)),

time: 43.9 us -> 43.9 us (level)
  no operation moved by 1% of the time
where the time goes in v6:
time: 43.9 us; the launch traced here: 43.8 us
  Pallas kernels  43.1 us (98%)
  between operations  0.64 us (1%)
    pallas_call x1, Pallas kernels, per_device(): pl.pallas_call(kernel, out_shape=tuple((pltpu.VMEM(shape, F32) for shape...  41.8 us
    pallas_call x1, Pallas kernels, per_device(): pl.pallas_call(write_out, out_shape=tuple((pltpu.HBM(shape, F32) for shap...  1.33 us

profile of v6, /device:TPU:8, one launch (start us, length us, event | category | flops | bytes accessed | tf_op | source)
XLA Modules:
  0.0 43.8 jit_solution(499035957530192900)
XLA Ops:
  0.6 41.8 %shard_map.50 = (f32[1,64,4096]{2,1,0:T(8,128)S(1)}, f32[64,4096]{1,0:T(8,128)S(1)}) custom-call(bf16[1,64,32768]{2,1,0:T(8,128)(2,1)} %raw.1, f32[1,64,4096]{2,1,0:T(8,128)} %mom.1, s32[32,64]{1,0:T(8,128)} %bitcast.1), custom_call_target="tpu_custom_call" | custom-call | tf_op jit(solution)/shard_map/pallas_call | solution.py:566
  42.4 1.3 %shard_map.51 = (f32[1,64,4096]{2,1,0:T(8,128)}, f32[64,4096]{1,0:T(8,128)}) custom-call(f32[1,64,4096]{2,1,0:T(8,128)S(1)} %get-tuple-element.4.new_m, f32[64,4096]{1,0:T(8,128)S(1)} %get-tuple-element.5.new_u), custom_call_target="tpu_custom_call" | custom-call | tf_op jit(solution)/shard_map/pallas_call | solution.py:602

commit v7 on v6

--- a/solution.py
+++ b/solution.py
@@ -159,7 +159,12 @@
 
     raw_copy(ACROSS, 1).wait()
 
-    @pl.loop(0, HALF)
+    widen(ACROSS, 0)
+    x_copy(ACROSS, 0).start()
+    widen(ACROSS, PIECES - 1)
+    x_copy(ACROSS, PIECES - 1).start()
+
+    @pl.loop(1, HALF)
     def _(i):
         for p in (i, PIECES - 1 - i):
             widen(ACROSS, p)

time: 43.9 us -> 43.9 us (level)
  no operation moved by 1% of the time
where the time goes in v7:
time: 43.9 us; the launch traced here: 43.8 us
  Pallas kernels  43.1 us (98%)
  between operations  0.64 us (1%)
    pallas_call x1, Pallas kernels, per_device(): pl.pallas_call(kernel, out_shape=tuple((pltpu.VMEM(shape, F32) for shape...  41.8 us
    pallas_call x1, Pallas kernels, per_device(): pl.pallas_call(write_out, out_shape=tuple((pltpu.HBM(shape, F32) for shap...  1.33 us

profile of v7, /device:TPU:8, one launch (start us, length us, event | category | flops | bytes accessed | tf_op | source)
XLA Modules:
  0.0 43.8 jit_solution(6743753857475031731)
XLA Ops:
  0.6 41.8 %shard_map.50 = (f32[1,64,4096]{2,1,0:T(8,128)S(1)}, f32[64,4096]{1,0:T(8,128)S(1)}) custom-call(bf16[1,64,32768]{2,1,0:T(8,128)(2,1)} %raw.1, f32[1,64,4096]{2,1,0:T(8,128)} %mom.1, s32[32,64]{1,0:T(8,128)} %bitcast.1), custom_call_target="tpu_custom_call" | custom-call | tf_op jit(solution)/shard_map/pallas_call | solution.py:571
  42.4 1.3 %shard_map.51 = (f32[1,64,4096]{2,1,0:T(8,128)}, f32[64,4096]{1,0:T(8,128)}) custom-call(f32[1,64,4096]{2,1,0:T(8,128)S(1)} %get-tuple-element.4.new_m, f32[64,4096]{1,0:T(8,128)S(1)} %get-tuple-element.5.new_u), custom_call_target="tpu_custom_call" | custom-call | tf_op jit(solution)/shard_map/pallas_call | solution.py:607

commit v8 on v7

--- a/solution.py
+++ b/solution.py
@@ -439,6 +439,7 @@
         pair_copy(0).wait_recv()
         for step in X_STEPS:
             rx_copy(step).start()
+        send_rest()
 
     def inverse(p, q, column):
         high, low = split(column * right[0, p, 64 * q:64 * q + 64, :])
@@ -455,7 +456,6 @@
     def _():
         for step in range(1, X):
             rx_copy(step).wait_recv()
-        send_rest()
         zslots[z] = (xslots[0] + xslots[1]) + (xslots[2] + xslots[3])
         for step in Z_STEPS:
             rz_copy(step).start()

time: 43.9 us -> 43.9 us (level)
  no operation moved by 1% of the time
where the time goes in v8:
time: 43.9 us; the launch traced here: 43.8 us
  Pallas kernels  43.1 us (98%)
  between operations  0.64 us (1%)
    pallas_call x1, Pallas kernels, per_device(): pl.pallas_call(kernel, out_shape=tuple((pltpu.VMEM(shape, F32) for shape...  41.8 us
    pallas_call x1, Pallas kernels, per_device(): pl.pallas_call(write_out, out_shape=tuple((pltpu.HBM(shape, F32) for shap...  1.33 us

profile of v8, /device:TPU:8, one launch (start us, length us, event | category | flops | bytes accessed | tf_op | source)
XLA Modules:
  0.0 43.8 jit_solution(15602170965426877279)
XLA Ops:
  0.6 41.8 %shard_map.50 = (f32[1,64,4096]{2,1,0:T(8,128)S(1)}, f32[64,4096]{1,0:T(8,128)S(1)}) custom-call(bf16[1,64,32768]{2,1,0:T(8,128)(2,1)} %raw.1, f32[1,64,4096]{2,1,0:T(8,128)} %mom.1, s32[32,64]{1,0:T(8,128)} %bitcast.1), custom_call_target="tpu_custom_call" | custom-call | tf_op jit(solution)/shard_map/pallas_call | solution.py:571
  42.4 1.3 %shard_map.51 = (f32[1,64,4096]{2,1,0:T(8,128)}, f32[64,4096]{1,0:T(8,128)}) custom-call(f32[1,64,4096]{2,1,0:T(8,128)S(1)} %get-tuple-element.4.new_m, f32[64,4096]{1,0:T(8,128)S(1)} %get-tuple-element.5.new_u), custom_call_target="tpu_custom_call" | custom-call | tf_op jit(solution)/shard_map/pallas_call | solution.py:607
